TPU v7x, 768 devices: a whole 4x8x12 slice. The times are simulated.
768 devices in a mesh: tok: 192 (over z, y, core), wid: 4 (over x).
Axes of the slice: x: 4, y: 8, z: 12, core: 2. Of those that a mesh axis runs over, the one named last changes fastest.
Arguments:
- activations: bfloat16 [49152, 8192], P('tok', 'wid'), may hold values from -180 to 180
- sketch: bfloat16 [8192, 256], P('wid'), may hold values from -6 to 6
Outputs:
- new_basis: bfloat16 [8192, 256], P('wid')
All inputs are finite; a program needn't handle non-finite values.
Results may differ from a plain program's by a relative error of at most 0.0034.
Values may be sent and summed in bfloat16 or wider, within the bound.
No kernel may reach another device: no remote copies, remote signals or barrier semaphores. Data moves between devices by JAX's collectives and lax.ppermute only.
A program may use at most 32 MiB of HBM per device.

v0:
```python
import math

import jax
import jax.numpy as jnp
from jax import lax
from jax.sharding import PartitionSpec as P

D = 8192


def on_device(activations, sketch):
    tok_rows, panel = activations.shape
    groups = lax.axis_size("tok")
    owned_rows = -(-panel // groups)
    padded = owned_rows * groups
    partial_sum = jnp.dot(activations, sketch, preferred_element_type=jnp.float32)
    summed = lax.psum(partial_sum, "wid")
    projected = (summed * (1.0 / math.sqrt(D))).astype(jnp.bfloat16)
    widened = jnp.pad(activations, ((0, 0), (0, padded - panel)))
    owned = lax.psum_scatter(
        lax.dot_general(
            widened, projected, (((0,), (0,)), ((), ())), preferred_element_type=jnp.float32
        ),
        "tok",
        scatter_dimension=0,
        tiled=True,
    ) / (tok_rows * groups)
    local_gram = lax.dot_general(
        owned, owned, (((0,), (0,)), ((), ())), precision=lax.Precision.HIGHEST
    )
    gram = lax.psum(local_gram, ("tok", "wid"))
    lower = jnp.linalg.cholesky(gram)
    solved = lax.linalg.triangular_solve(
        lower, owned, left_side=False, lower=True, transpose_a=True
    )
    rows_new = (solved * math.sqrt(D)).astype(jnp.bfloat16)
    gathered = lax.all_gather(rows_new, "tok", axis=0, tiled=True)
    return gathered[:panel]


def solution(mesh):
    placed = (P("tok", "wid"), P("wid", None))
    return jax.shard_map(
        on_device, mesh=mesh, in_specs=placed, out_specs=P("wid", None), check_vma=False
    )
```

profile of v0, /device:TPU:1, one launch (start us, length us, event | category | flops | bytes accessed | tf_op | source)
XLA Modules:
  0.0 1740.4 jit_solution(11317182415700332236)
XLA Ops:
  7.8 2.4 fusion.18
  10.2 63.8 %all-reduce.7.cloned.1.call-done = f32[256,256]{1,0:T(8,128)} async-done(((f32[256,256]{1,0:T(8,128)}), f32[256,256]{1,0:T(8,128)}) %all-reduce.7.cloned.1.call-update) | async-done | bytes 262160 | tf_op jit(solution)/shard_map/psum | solution.py:17
  74.0 1.8 fusion.1
  75.7 424.3 %fusion = f32[16,256]{1,0:T(8,128)S(1)} fusion(f32[2112,256]{1,0:T(8,128)S(1)} %fusion.1), kind=kCustom, calls=%all-reduce-scatter | all-reduce-scatter fusion | flops 786433 | bytes 2183168
  501.4 1.3 collective-permute-start.57
  502.7 1.3 collective-permute-start.56
  504.0 1.3 collective-permute-start.55
  505.3 1.3 collective-permute-start.59
  508.7 1.3 collective-permute-start.53
  514.0 1.3 collective-permute-start.49
  517.9 1.3 collective-permute-start.46
  519.2 27.2 %collective-permute-start.45 = (f32[16,256]{1,0:T(8,128)S(1)}, f32[16,256]{1,0:T(8,128)S(1)}, u32[]{:S(2)}, u32[]{:S(2)}) collective-permute-start(f32[16,256]{1,0:T(8,128)S(1)} %fusion), channel_id=1, source_target_pairs={{0,184},{4,188},{8,192},{12,196},{16,200},{20,204},{24,208},{28,21... | collective-permute-start | bytes 49160
  546.5 5.3 collective-permute-start.44
  551.8 5.0 collective-permute-start.43
  556.8 4.4 collective-permute-start.42
  561.2 3.2 collective-permute-start.41
  564.4 2.8 collective-permute-start.40
  567.2 1.5 collective-permute-start.39
  568.7 4.8 collective-permute-start.38
  576.1 1.3 collective-permute-start.35
  578.8 3.4 collective-permute-start.33
  583.4 2.0 collective-permute-start.31
  585.4 2.5 collective-permute-start.30
  588.0 3.4 collective-permute-start.29
  591.4 2.8 collective-permute-start.28
  595.6 3.9 collective-permute-start.26
  599.5 3.2 collective-permute-start.25
  602.7 4.0 collective-permute-start.24
  606.7 5.6 collective-permute-start.23
  612.3 20.5 %collective-permute-start.22 = (f32[16,256]{1,0:T(8,128)S(1)}, f32[16,256]{1,0:T(8,128)S(1)}, u32[]{:S(2)}, u32[]{:S(2)}) collective-permute-start(f32[16,256]{1,0:T(8,128)S(1)} %fusion), channel_id=1, source_target_pairs={{0,92},{4,96},{8,100},{12,104},{16,108},{20,112},{24,116},{28,120}... | collective-permute-start | bytes 49160
  632.7 20.5 %collective-permute-start.21 = (f32[16,256]{1,0:T(8,128)S(1)}, f32[16,256]{1,0:T(8,128)S(1)}, u32[]{:S(2)}, u32[]{:S(2)}) collective-permute-start(f32[16,256]{1,0:T(8,128)S(1)} %fusion), channel_id=1, source_target_pairs={{0,88},{4,92},{8,96},{12,100},{16,104},{20,108},{24,112},{28,116},... | collective-permute-start | bytes 49160
  653.2 20.5 %collective-permute-start.20 = (f32[16,256]{1,0:T(8,128)S(1)}, f32[16,256]{1,0:T(8,128)S(1)}, u32[]{:S(2)}, u32[]{:S(2)}) collective-permute-start(f32[16,256]{1,0:T(8,128)S(1)} %fusion), channel_id=1, source_target_pairs={{0,84},{4,88},{8,92},{12,96},{16,100},{20,104},{24,108},{28,112},{... | collective-permute-start | bytes 49160
  673.7 20.5 %collective-permute-start.19 = (f32[16,256]{1,0:T(8,128)S(1)}, f32[16,256]{1,0:T(8,128)S(1)}, u32[]{:S(2)}, u32[]{:S(2)}) collective-permute-start(f32[16,256]{1,0:T(8,128)S(1)} %fusion), channel_id=1, source_target_pairs={{0,80},{4,84},{8,88},{12,92},{16,96},{20,100},{24,104},{28,108},{3... | collective-permute-start | bytes 49160
  694.2 20.5 %collective-permute-start.18 = (f32[16,256]{1,0:T(8,128)S(1)}, f32[16,256]{1,0:T(8,128)S(1)}, u32[]{:S(2)}, u32[]{:S(2)}) collective-permute-start(f32[16,256]{1,0:T(8,128)S(1)} %fusion), channel_id=1, source_target_pairs={{0,76},{4,80},{8,84},{12,88},{16,92},{20,96},{24,100},{28,104},{32... | collective-permute-start | bytes 49160
  714.7 20.5 %collective-permute-start.17 = (f32[16,256]{1,0:T(8,128)S(1)}, f32[16,256]{1,0:T(8,128)S(1)}, u32[]{:S(2)}, u32[]{:S(2)}) collective-permute-start(f32[16,256]{1,0:T(8,128)S(1)} %fusion), channel_id=1, source_target_pairs={{0,72},{4,76},{8,80},{12,84},{16,88},{20,92},{24,96},{28,100},{32,... | collective-permute-start | bytes 49160
  735.1 20.5 %collective-permute-start.16 = (f32[16,256]{1,0:T(8,128)S(1)}, f32[16,256]{1,0:T(8,128)S(1)}, u32[]{:S(2)}, u32[]{:S(2)}) collective-permute-start(f32[16,256]{1,0:T(8,128)S(1)} %fusion), channel_id=1, source_target_pairs={{0,68},{4,72},{8,76},{12,80},{16,84},{20,88},{24,92},{28,96},{32,1... | collective-permute-start | bytes 49160
  755.6 20.5 %collective-permute-start.15 = (f32[16,256]{1,0:T(8,128)S(1)}, f32[16,256]{1,0:T(8,128)S(1)}, u32[]{:S(2)}, u32[]{:S(2)}) collective-permute-start(f32[16,256]{1,0:T(8,128)S(1)} %fusion), channel_id=1, source_target_pairs={{0,64},{4,68},{8,72},{12,76},{16,80},{20,84},{24,88},{28,92},{32,9... | collective-permute-start | bytes 49160
  776.1 20.5 %collective-permute-start.14 = (f32[16,256]{1,0:T(8,128)S(1)}, f32[16,256]{1,0:T(8,128)S(1)}, u32[]{:S(2)}, u32[]{:S(2)}) collective-permute-start(f32[16,256]{1,0:T(8,128)S(1)} %fusion), channel_id=1, source_target_pairs={{0,60},{4,64},{8,68},{12,72},{16,76},{20,80},{24,84},{28,88},{32,9... | collective-permute-start | bytes 49160
  796.6 20.5 %collective-permute-start.13 = (f32[16,256]{1,0:T(8,128)S(1)}, f32[16,256]{1,0:T(8,128)S(1)}, u32[]{:S(2)}, u32[]{:S(2)}) collective-permute-start(f32[16,256]{1,0:T(8,128)S(1)} %fusion), channel_id=1, source_target_pairs={{0,56},{4,60},{8,64},{12,68},{16,72},{20,76},{24,80},{28,84},{32,8... | collective-permute-start | bytes 49160
  817.1 20.5 %collective-permute-start.12 = (f32[16,256]{1,0:T(8,128)S(1)}, f32[16,256]{1,0:T(8,128)S(1)}, u32[]{:S(2)}, u32[]{:S(2)}) collective-permute-start(f32[16,256]{1,0:T(8,128)S(1)} %fusion), channel_id=1, source_target_pairs={{0,52},{4,56},{8,60},{12,64},{16,68},{20,72},{24,76},{28,80},{32,8... | collective-permute-start | bytes 49160
  837.6 20.5 %collective-permute-start.11 = (f32[16,256]{1,0:T(8,128)S(1)}, f32[16,256]{1,0:T(8,128)S(1)}, u32[]{:S(2)}, u32[]{:S(2)}) collective-permute-start(f32[16,256]{1,0:T(8,128)S(1)} %fusion), channel_id=1, source_target_pairs={{0,48},{4,52},{8,56},{12,60},{16,64},{20,68},{24,72},{28,76},{32,8... | collective-permute-start | bytes 49160
  858.0 20.5 %collective-permute-start.10 = (f32[16,256]{1,0:T(8,128)S(1)}, f32[16,256]{1,0:T(8,128)S(1)}, u32[]{:S(2)}, u32[]{:S(2)}) collective-permute-start(f32[16,256]{1,0:T(8,128)S(1)} %fusion), channel_id=1, source_target_pairs={{0,44},{4,48},{8,52},{12,56},{16,60},{20,64},{24,68},{28,72},{32,7... | collective-permute-start | bytes 49160
  878.5 20.5 %collective-permute-start.9 = (f32[16,256]{1,0:T(8,128)S(1)}, f32[16,256]{1,0:T(8,128)S(1)}, u32[]{:S(2)}, u32[]{:S(2)}) collective-permute-start(f32[16,256]{1,0:T(8,128)S(1)} %fusion), channel_id=1, source_target_pairs={{0,40},{4,44},{8,48},{12,52},{16,56},{20,60},{24,64},{28,68},{32,7... | collective-permute-start | bytes 49160
  899.0 20.5 %collective-permute-start.8 = (f32[16,256]{1,0:T(8,128)S(1)}, f32[16,256]{1,0:T(8,128)S(1)}, u32[]{:S(2)}, u32[]{:S(2)}) collective-permute-start(f32[16,256]{1,0:T(8,128)S(1)} %fusion), channel_id=1, source_target_pairs={{0,36},{4,40},{8,44},{12,48},{16,52},{20,56},{24,60},{28,64},{32,6... | collective-permute-start | bytes 49160
  919.5 20.5 %collective-permute-start.7 = (f32[16,256]{1,0:T(8,128)S(1)}, f32[16,256]{1,0:T(8,128)S(1)}, u32[]{:S(2)}, u32[]{:S(2)}) collective-permute-start(f32[16,256]{1,0:T(8,128)S(1)} %fusion), channel_id=1, source_target_pairs={{0,32},{4,36},{8,40},{12,44},{16,48},{20,52},{24,56},{28,60},{32,6... | collective-permute-start | bytes 49160
  940.0 20.5 %collective-permute-start.6 = (f32[16,256]{1,0:T(8,128)S(1)}, f32[16,256]{1,0:T(8,128)S(1)}, u32[]{:S(2)}, u32[]{:S(2)}) collective-permute-start(f32[16,256]{1,0:T(8,128)S(1)} %fusion), channel_id=1, source_target_pairs={{0,28},{4,32},{8,36},{12,40},{16,44},{20,48},{24,52},{28,56},{32,6... | collective-permute-start | bytes 49160
  960.5 20.5 %collective-permute-start.5 = (f32[16,256]{1,0:T(8,128)S(1)}, f32[16,256]{1,0:T(8,128)S(1)}, u32[]{:S(2)}, u32[]{:S(2)}) collective-permute-start(f32[16,256]{1,0:T(8,128)S(1)} %fusion), channel_id=1, source_target_pairs={{0,24},{4,28},{8,32},{12,36},{16,40},{20,44},{24,48},{28,52},{32,5... | collective-permute-start | bytes 49160
  980.9 20.5 %collective-permute-start.4 = (f32[16,256]{1,0:T(8,128)S(1)}, f32[16,256]{1,0:T(8,128)S(1)}, u32[]{:S(2)}, u32[]{:S(2)}) collective-permute-start(f32[16,256]{1,0:T(8,128)S(1)} %fusion), channel_id=1, source_target_pairs={{0,20},{4,24},{8,28},{12,32},{16,36},{20,40},{24,44},{28,48},{32,5... | collective-permute-start | bytes 49160
  1001.4 20.5 %collective-permute-start.3 = (f32[16,256]{1,0:T(8,128)S(1)}, f32[16,256]{1,0:T(8,128)S(1)}, u32[]{:S(2)}, u32[]{:S(2)}) collective-permute-start(f32[16,256]{1,0:T(8,128)S(1)} %fusion), channel_id=1, source_target_pairs={{0,16},{4,20},{8,24},{12,28},{16,32},{20,36},{24,40},{28,44},{32,4... | collective-permute-start | bytes 49160
  1021.9 20.5 %collective-permute-start.2 = (f32[16,256]{1,0:T(8,128)S(1)}, f32[16,256]{1,0:T(8,128)S(1)}, u32[]{:S(2)}, u32[]{:S(2)}) collective-permute-start(f32[16,256]{1,0:T(8,128)S(1)} %fusion), channel_id=1, source_target_pairs={{0,12},{4,16},{8,20},{12,24},{16,28},{20,32},{24,36},{28,40},{32,4... | collective-permute-start | bytes 49160
  1042.4 20.5 %collective-permute-start.1 = (f32[16,256]{1,0:T(8,128)S(1)}, f32[16,256]{1,0:T(8,128)S(1)}, u32[]{:S(2)}, u32[]{:S(2)}) collective-permute-start(f32[16,256]{1,0:T(8,128)S(1)} %fusion), channel_id=1, source_target_pairs={{0,8},{4,12},{8,16},{12,20},{16,24},{20,28},{24,32},{28,36},{32,40... | collective-permute-start | bytes 49160
  1062.9 20.5 %collective-permute-start = (f32[16,256]{1,0:T(8,128)S(1)}, f32[16,256]{1,0:T(8,128)S(1)}, u32[]{:S(2)}, u32[]{:S(2)}) collective-permute-start(f32[16,256]{1,0:T(8,128)S(1)} %fusion), channel_id=1, source_target_pairs={{0,4},{4,8},{8,12},{12,16},{16,20},{20,24},{24,28},{28,32},{32,36}... | collective-permute-start | bytes 49160
  1085.3 5.0 collective-permute-done
  1090.3 6.8 concatenate.3
  1098.5 459.7 %all-reduce.9.cloned.1.call-done = f32[256,256]{0,1:T(8,128)} async-done(((f32[256,256]{0,1:T(8,128)}), f32[256,256]{0,1:T(8,128)}) %all-reduce.9.cloned.1.call-update) | async-done | bytes 262160 | tf_op jit(solution)/shard_map/psum | solution.py:31
  1560.3 11.7 cholesky.50
  1572.0 9.8 custom-call.14
  1582.4 11.7 cholesky.105
  1596.1 4.1 while.1
  1596.9 1.3 bitcast_dynamic-update-slice_fusion.2
  1598.9 1.3 bitcast_dynamic-update-slice_fusion.2
  1600.2 19.7 %custom-call.15 = f32[2,128,128]{1,2,0:T(8,128)S(1)} custom-call(f32[2,128,128]{2,1,0:T(8,128)S(1)} %get-tuple-element.12), custom_call_target="InvertDiagBlocksLowerTriangular" | custom-call | tf_op jit(solution)/shard_map/triangular_solve | solution.py:33
  1621.1 109.4 %all-gather.3.cloned.1.call-done = bf16[192,11,256]{2,1,0:T(8,128)(2,1)} async-done(((bf16[1,11,256]{2,1,0:T(8,128)(2,1)}), bf16[192,11,256]{2,1,0:T(8,128)(2,1)}) %all-gather.3.cloned.1.call-update) | async-done | bytes 1081360 | tf_op jit(solution)/shard_map/all_gather | solution.py:37
  1730.5 2.3 reshape.37
  (105 shorter events, 27.2 us)
Async XLA Ops:
  6.5 1.2 copy-start
  6.5 67.4 %all-reduce.7.cloned.1.call-start = ((), (), s32[]{:S(2)}) async-start(), calls=%async_computation | async-start | bytes 524288 | tf_op jit(solution)/shard_map/psum | solution.py:17
  10.1 1548.0 %all-reduce.9.cloned.1.call-start = ((), (), s32[]{:S(2)}) async-start(), calls=%async_computation.1 | async-start | bytes 524288 | tf_op jit(solution)/shard_map/psum | solution.py:31
  500.1 8.6 collective-permute-start.58
  501.4 8.7 collective-permute-start.57
  502.7 8.7 collective-permute-start.56
  504.0 8.7 collective-permute-start.55
  505.3 2.1 collective-permute-start.59
  507.4 6.5 collective-permute-start.54
  508.7 6.5 collective-permute-start.53
  510.0 6.5 collective-permute-start.52
  511.3 6.5 collective-permute-start.51
  512.7 6.5 collective-permute-start.50
  514.0 32.5 %collective-permute-start.49 = (f32[16,256]{1,0:T(8,128)S(1)}, f32[16,256]{1,0:T(8,128)S(1)}, u32[]{:S(2)}, u32[]{:S(2)}) collective-permute-start(f32[16,256]{1,0:T(8,128)S(1)} %fusion), channel_id=1, source_target_pairs={{0,200},{4,204},{8,208},{12,212},{16,216},{20,220},{24,224},{28,22... | collective-permute-start | bytes 49160
  515.3 36.5 %collective-permute-start.48 = (f32[16,256]{1,0:T(8,128)S(1)}, f32[16,256]{1,0:T(8,128)S(1)}, u32[]{:S(2)}, u32[]{:S(2)}) collective-permute-start(f32[16,256]{1,0:T(8,128)S(1)} %fusion), channel_id=1, source_target_pairs={{0,196},{4,200},{8,204},{12,208},{16,212},{20,216},{24,220},{28,22... | collective-permute-start | bytes 49160
  516.6 40.2 %collective-permute-start.47 = (f32[16,256]{1,0:T(8,128)S(1)}, f32[16,256]{1,0:T(8,128)S(1)}, u32[]{:S(2)}, u32[]{:S(2)}) collective-permute-start(f32[16,256]{1,0:T(8,128)S(1)} %fusion), channel_id=1, source_target_pairs={{0,192},{4,196},{8,200},{12,204},{16,208},{20,212},{24,216},{28,22... | collective-permute-start | bytes 49160
  517.9 43.4 %collective-permute-start.46 = (f32[16,256]{1,0:T(8,128)S(1)}, f32[16,256]{1,0:T(8,128)S(1)}, u32[]{:S(2)}, u32[]{:S(2)}) collective-permute-start(f32[16,256]{1,0:T(8,128)S(1)} %fusion), channel_id=1, source_target_pairs={{0,188},{4,192},{8,196},{12,200},{16,204},{20,208},{24,212},{28,21... | collective-permute-start | bytes 49160
  519.2 45.2 %collective-permute-start.45 = (f32[16,256]{1,0:T(8,128)S(1)}, f32[16,256]{1,0:T(8,128)S(1)}, u32[]{:S(2)}, u32[]{:S(2)}) collective-permute-start(f32[16,256]{1,0:T(8,128)S(1)} %fusion), channel_id=1, source_target_pairs={{0,184},{4,188},{8,192},{12,196},{16,200},{20,204},{24,208},{28,21... | collective-permute-start | bytes 49160
  546.5 20.8 %collective-permute-start.44 = (f32[16,256]{1,0:T(8,128)S(1)}, f32[16,256]{1,0:T(8,128)S(1)}, u32[]{:S(2)}, u32[]{:S(2)}) collective-permute-start(f32[16,256]{1,0:T(8,128)S(1)} %fusion), channel_id=1, source_target_pairs={{0,180},{4,184},{8,188},{12,192},{16,196},{20,200},{24,204},{28,20... | collective-permute-start | bytes 49160
  551.8 16.9 collective-permute-start.43
  556.8 16.7 collective-permute-start.42
  561.2 13.6 collective-permute-start.41
  564.4 11.7 collective-permute-start.40
  567.2 10.2 collective-permute-start.39
  568.7 10.0 collective-permute-start.38
  573.5 8.6 collective-permute-start.37
  574.8 8.6 collective-permute-start.36
  576.1 9.3 collective-permute-start.35
  577.4 10.5 collective-permute-start.34
  578.8 12.7 collective-permute-start.33
  582.1 12.1 collective-permute-start.32
  583.4 12.1 collective-permute-start.31
  585.4 14.0 collective-permute-start.30
  588.0 14.7 collective-permute-start.29
  591.4 15.2 collective-permute-start.28
  594.3 18.0 %collective-permute-start.27 = (f32[16,256]{1,0:T(8,128)S(1)}, f32[16,256]{1,0:T(8,128)S(1)}, u32[]{:S(2)}, u32[]{:S(2)}) collective-permute-start(f32[16,256]{1,0:T(8,128)S(1)} %fusion), channel_id=1, source_target_pairs={{0,112},{4,116},{8,120},{12,124},{16,128},{20,132},{24,136},{28,14... | collective-permute-start | bytes 49160
  595.6 37.2 %collective-permute-start.26 = (f32[16,256]{1,0:T(8,128)S(1)}, f32[16,256]{1,0:T(8,128)S(1)}, u32[]{:S(2)}, u32[]{:S(2)}) collective-permute-start(f32[16,256]{1,0:T(8,128)S(1)} %fusion), channel_id=1, source_target_pairs={{0,108},{4,112},{8,116},{12,120},{16,124},{20,128},{24,132},{28,13... | collective-permute-start | bytes 49160
  599.5 53.8 %collective-permute-start.25 = (f32[16,256]{1,0:T(8,128)S(1)}, f32[16,256]{1,0:T(8,128)S(1)}, u32[]{:S(2)}, u32[]{:S(2)}) collective-permute-start(f32[16,256]{1,0:T(8,128)S(1)} %fusion), channel_id=1, source_target_pairs={{0,104},{4,108},{8,112},{12,116},{16,120},{20,124},{24,128},{28,13... | collective-permute-start | bytes 49160
  602.7 71.0 %collective-permute-start.24 = (f32[16,256]{1,0:T(8,128)S(1)}, f32[16,256]{1,0:T(8,128)S(1)}, u32[]{:S(2)}, u32[]{:S(2)}) collective-permute-start(f32[16,256]{1,0:T(8,128)S(1)} %fusion), channel_id=1, source_target_pairs={{0,100},{4,104},{8,108},{12,112},{16,116},{20,120},{24,124},{28,12... | collective-permute-start | bytes 49160
  606.7 87.5 %collective-permute-start.23 = (f32[16,256]{1,0:T(8,128)S(1)}, f32[16,256]{1,0:T(8,128)S(1)}, u32[]{:S(2)}, u32[]{:S(2)}) collective-permute-start(f32[16,256]{1,0:T(8,128)S(1)} %fusion), channel_id=1, source_target_pairs={{0,96},{4,100},{8,104},{12,108},{16,112},{20,116},{24,120},{28,124... | collective-permute-start | bytes 49160
  612.3 102.4 %collective-permute-start.22 = (f32[16,256]{1,0:T(8,128)S(1)}, f32[16,256]{1,0:T(8,128)S(1)}, u32[]{:S(2)}, u32[]{:S(2)}) collective-permute-start(f32[16,256]{1,0:T(8,128)S(1)} %fusion), channel_id=1, source_target_pairs={{0,92},{4,96},{8,100},{12,104},{16,108},{20,112},{24,116},{28,120}... | collective-permute-start | bytes 49160
  632.7 102.4 %collective-permute-start.21 = (f32[16,256]{1,0:T(8,128)S(1)}, f32[16,256]{1,0:T(8,128)S(1)}, u32[]{:S(2)}, u32[]{:S(2)}) collective-permute-start(f32[16,256]{1,0:T(8,128)S(1)} %fusion), channel_id=1, source_target_pairs={{0,88},{4,92},{8,96},{12,100},{16,104},{20,108},{24,112},{28,116},... | collective-permute-start | bytes 49160
  653.2 102.4 %collective-permute-start.20 = (f32[16,256]{1,0:T(8,128)S(1)}, f32[16,256]{1,0:T(8,128)S(1)}, u32[]{:S(2)}, u32[]{:S(2)}) collective-permute-start(f32[16,256]{1,0:T(8,128)S(1)} %fusion), channel_id=1, source_target_pairs={{0,84},{4,88},{8,92},{12,96},{16,100},{20,104},{24,108},{28,112},{... | collective-permute-start | bytes 49160
  673.7 102.4 %collective-permute-start.19 = (f32[16,256]{1,0:T(8,128)S(1)}, f32[16,256]{1,0:T(8,128)S(1)}, u32[]{:S(2)}, u32[]{:S(2)}) collective-permute-start(f32[16,256]{1,0:T(8,128)S(1)} %fusion), channel_id=1, source_target_pairs={{0,80},{4,84},{8,88},{12,92},{16,96},{20,100},{24,104},{28,108},{3... | collective-permute-start | bytes 49160
  694.2 102.4 %collective-permute-start.18 = (f32[16,256]{1,0:T(8,128)S(1)}, f32[16,256]{1,0:T(8,128)S(1)}, u32[]{:S(2)}, u32[]{:S(2)}) collective-permute-start(f32[16,256]{1,0:T(8,128)S(1)} %fusion), channel_id=1, source_target_pairs={{0,76},{4,80},{8,84},{12,88},{16,92},{20,96},{24,100},{28,104},{32... | collective-permute-start | bytes 49160
  714.7 102.4 %collective-permute-start.17 = (f32[16,256]{1,0:T(8,128)S(1)}, f32[16,256]{1,0:T(8,128)S(1)}, u32[]{:S(2)}, u32[]{:S(2)}) collective-permute-start(f32[16,256]{1,0:T(8,128)S(1)} %fusion), channel_id=1, source_target_pairs={{0,72},{4,76},{8,80},{12,84},{16,88},{20,92},{24,96},{28,100},{32,... | collective-permute-start | bytes 49160
  735.1 102.4 %collective-permute-start.16 = (f32[16,256]{1,0:T(8,128)S(1)}, f32[16,256]{1,0:T(8,128)S(1)}, u32[]{:S(2)}, u32[]{:S(2)}) collective-permute-start(f32[16,256]{1,0:T(8,128)S(1)} %fusion), channel_id=1, source_target_pairs={{0,68},{4,72},{8,76},{12,80},{16,84},{20,88},{24,92},{28,96},{32,1... | collective-permute-start | bytes 49160
  755.6 102.4 %collective-permute-start.15 = (f32[16,256]{1,0:T(8,128)S(1)}, f32[16,256]{1,0:T(8,128)S(1)}, u32[]{:S(2)}, u32[]{:S(2)}) collective-permute-start(f32[16,256]{1,0:T(8,128)S(1)} %fusion), channel_id=1, source_target_pairs={{0,64},{4,68},{8,72},{12,76},{16,80},{20,84},{24,88},{28,92},{32,9... | collective-permute-start | bytes 49160
  776.1 102.4 %collective-permute-start.14 = (f32[16,256]{1,0:T(8,128)S(1)}, f32[16,256]{1,0:T(8,128)S(1)}, u32[]{:S(2)}, u32[]{:S(2)}) collective-permute-start(f32[16,256]{1,0:T(8,128)S(1)} %fusion), channel_id=1, source_target_pairs={{0,60},{4,64},{8,68},{12,72},{16,76},{20,80},{24,84},{28,88},{32,9... | collective-permute-start | bytes 49160
  796.6 102.4 %collective-permute-start.13 = (f32[16,256]{1,0:T(8,128)S(1)}, f32[16,256]{1,0:T(8,128)S(1)}, u32[]{:S(2)}, u32[]{:S(2)}) collective-permute-start(f32[16,256]{1,0:T(8,128)S(1)} %fusion), channel_id=1, source_target_pairs={{0,56},{4,60},{8,64},{12,68},{16,72},{20,76},{24,80},{28,84},{32,8... | collective-permute-start | bytes 49160
  817.1 102.4 %collective-permute-start.12 = (f32[16,256]{1,0:T(8,128)S(1)}, f32[16,256]{1,0:T(8,128)S(1)}, u32[]{:S(2)}, u32[]{:S(2)}) collective-permute-start(f32[16,256]{1,0:T(8,128)S(1)} %fusion), channel_id=1, source_target_pairs={{0,52},{4,56},{8,60},{12,64},{16,68},{20,72},{24,76},{28,80},{32,8... | collective-permute-start | bytes 49160
  837.6 102.4 %collective-permute-start.11 = (f32[16,256]{1,0:T(8,128)S(1)}, f32[16,256]{1,0:T(8,128)S(1)}, u32[]{:S(2)}, u32[]{:S(2)}) collective-permute-start(f32[16,256]{1,0:T(8,128)S(1)} %fusion), channel_id=1, source_target_pairs={{0,48},{4,52},{8,56},{12,60},{16,64},{20,68},{24,72},{28,76},{32,8... | collective-permute-start | bytes 49160
  858.0 102.4 %collective-permute-start.10 = (f32[16,256]{1,0:T(8,128)S(1)}, f32[16,256]{1,0:T(8,128)S(1)}, u32[]{:S(2)}, u32[]{:S(2)}) collective-permute-start(f32[16,256]{1,0:T(8,128)S(1)} %fusion), channel_id=1, source_target_pairs={{0,44},{4,48},{8,52},{12,56},{16,60},{20,64},{24,68},{28,72},{32,7... | collective-permute-start | bytes 49160
  878.5 102.4 %collective-permute-start.9 = (f32[16,256]{1,0:T(8,128)S(1)}, f32[16,256]{1,0:T(8,128)S(1)}, u32[]{:S(2)}, u32[]{:S(2)}) collective-permute-start(f32[16,256]{1,0:T(8,128)S(1)} %fusion), channel_id=1, source_target_pairs={{0,40},{4,44},{8,48},{12,52},{16,56},{20,60},{24,64},{28,68},{32,7... | collective-permute-start | bytes 49160
  899.0 102.4 %collective-permute-start.8 = (f32[16,256]{1,0:T(8,128)S(1)}, f32[16,256]{1,0:T(8,128)S(1)}, u32[]{:S(2)}, u32[]{:S(2)}) collective-permute-start(f32[16,256]{1,0:T(8,128)S(1)} %fusion), channel_id=1, source_target_pairs={{0,36},{4,40},{8,44},{12,48},{16,52},{20,56},{24,60},{28,64},{32,6... | collective-permute-start | bytes 49160
  919.5 102.4 %collective-permute-start.7 = (f32[16,256]{1,0:T(8,128)S(1)}, f32[16,256]{1,0:T(8,128)S(1)}, u32[]{:S(2)}, u32[]{:S(2)}) collective-permute-start(f32[16,256]{1,0:T(8,128)S(1)} %fusion), channel_id=1, source_target_pairs={{0,32},{4,36},{8,40},{12,44},{16,48},{20,52},{24,56},{28,60},{32,6... | collective-permute-start | bytes 49160
  940.0 102.4 %collective-permute-start.6 = (f32[16,256]{1,0:T(8,128)S(1)}, f32[16,256]{1,0:T(8,128)S(1)}, u32[]{:S(2)}, u32[]{:S(2)}) collective-permute-start(f32[16,256]{1,0:T(8,128)S(1)} %fusion), channel_id=1, source_target_pairs={{0,28},{4,32},{8,36},{12,40},{16,44},{20,48},{24,52},{28,56},{32,6... | collective-permute-start | bytes 49160
  960.5 102.4 %collective-permute-start.5 = (f32[16,256]{1,0:T(8,128)S(1)}, f32[16,256]{1,0:T(8,128)S(1)}, u32[]{:S(2)}, u32[]{:S(2)}) collective-permute-start(f32[16,256]{1,0:T(8,128)S(1)} %fusion), channel_id=1, source_target_pairs={{0,24},{4,28},{8,32},{12,36},{16,40},{20,44},{24,48},{28,52},{32,5... | collective-permute-start | bytes 49160
  980.9 104.3 %collective-permute-start.4 = (f32[16,256]{1,0:T(8,128)S(1)}, f32[16,256]{1,0:T(8,128)S(1)}, u32[]{:S(2)}, u32[]{:S(2)}) collective-permute-start(f32[16,256]{1,0:T(8,128)S(1)} %fusion), channel_id=1, source_target_pairs={{0,20},{4,24},{8,28},{12,32},{16,36},{20,40},{24,44},{28,48},{32,5... | collective-permute-start | bytes 49160
  1001.4 83.9 %collective-permute-start.3 = (f32[16,256]{1,0:T(8,128)S(1)}, f32[16,256]{1,0:T(8,128)S(1)}, u32[]{:S(2)}, u32[]{:S(2)}) collective-permute-start(f32[16,256]{1,0:T(8,128)S(1)} %fusion), channel_id=1, source_target_pairs={{0,16},{4,20},{8,24},{12,28},{16,32},{20,36},{24,40},{28,44},{32,4... | collective-permute-start | bytes 49160
  1021.9 63.4 %collective-permute-start.2 = (f32[16,256]{1,0:T(8,128)S(1)}, f32[16,256]{1,0:T(8,128)S(1)}, u32[]{:S(2)}, u32[]{:S(2)}) collective-permute-start(f32[16,256]{1,0:T(8,128)S(1)} %fusion), channel_id=1, source_target_pairs={{0,12},{4,16},{8,20},{12,24},{16,28},{20,32},{24,36},{28,40},{32,4... | collective-permute-start | bytes 49160
  1042.4 42.9 %collective-permute-start.1 = (f32[16,256]{1,0:T(8,128)S(1)}, f32[16,256]{1,0:T(8,128)S(1)}, u32[]{:S(2)}, u32[]{:S(2)}) collective-permute-start(f32[16,256]{1,0:T(8,128)S(1)} %fusion), channel_id=1, source_target_pairs={{0,8},{4,12},{8,16},{12,20},{16,24},{20,28},{24,32},{28,36},{32,40... | collective-permute-start | bytes 49160
  1062.9 27.5 %collective-permute-start = (f32[16,256]{1,0:T(8,128)S(1)}, f32[16,256]{1,0:T(8,128)S(1)}, u32[]{:S(2)}, u32[]{:S(2)}) collective-permute-start(f32[16,256]{1,0:T(8,128)S(1)} %fusion), channel_id=1, source_target_pairs={{0,4},{4,8},{8,12},{12,16},{16,20},{20,24},{24,28},{28,32},{32,36}... | collective-permute-start | bytes 49160
  1098.3 632.3 %all-gather.3.cloned.1.call-start = ((), (), s32[]{:S(2)}) async-start(), calls=%async_computation.2 | async-start | bytes 1581056 | tf_op jit(solution)/shard_map/all_gather | solution.py:37
Sparse Core Ops, SparseCore 0:
  10.3 63.6 all-reduce.6
  1098.4 459.7 all-reduce.8
  1621.2 109.2 all-gather.2
where the time goes:
time: 1740 us
  waiting for transfers between devices  639 us (37%)
  starting transfers between devices  582 us (33%)
  blocking collectives  424 us (24%)
  other arithmetic  55.3 us (3%)
  local copies, waits for them, and re-layouts  17.7 us (1%)
    unnamed x60, starting transfers between devices  581 us
    psum x1, waiting for transfers between devices, on_device(): gram = lax.psum(local_gram, ('tok', 'wid'))  460 us
    unnamed x1, blocking collectives  424 us
    all_gather x1, waiting for transfers between devices, on_device(): gathered = lax.all_gather(rows_new, 'tok', axis=0, tiled=True)  109 us
    psum x1, waiting for transfers between devices, on_device(): summed = lax.psum(partial_sum, 'wid')  63.8 us
  transfers between devices with their start and end apart: 63, of which 5 were waited for; matrix products, arithmetic and copies ran while one was open for 0% of the time, Pallas kernels for 0%

commit v1 on v0

v1 whole, which is shorter than its diff:
```python
import math

import jax
import jax.numpy as jnp
from jax import lax
from jax.experimental import pallas as pl
from jax.experimental.pallas import tpu as pltpu
from jax.sharding import Mesh, PartitionSpec as P

D = 8192
K = 256
TOKENS = 49152
BLOCK = 8
TOK = ("zh", "zl", "y", "core")


def inverse_factor_kernel(gram_ref, out_ref, work):
    work[...] = gram_ref[...]
    lane = lax.broadcasted_iota(jnp.int32, (BLOCK, K), 1)
    row_of = lax.broadcasted_iota(jnp.int32, (BLOCK, K), 0)
    for j in range(0, K, BLOCK):
        inside = (lane >= j) & (lane < j + BLOCK)
        rows = work[j : j + BLOCK, :]
        columns = [jnp.broadcast_to(rows[:, j + c : j + c + 1], (BLOCK, 128)) for c in range(BLOCK)]
        left = {
            (r, c): jnp.broadcast_to(columns[c][r : r + 1, :], (BLOCK, 128))
            for c in range(BLOCK)
            for r in range(c, BLOCK)
        }
        scale, low = [], {}
        for t in range(BLOCK):
            inv = lax.rsqrt(left[t, t])
            scale.append(jnp.concatenate([inv, inv], axis=1))
            narrow = {r: left[r, t] * inv for r in range(t + 1, BLOCK)}
            for c in range(t + 1, BLOCK):
                for r in range(c, BLOCK):
                    left[r, c] = left[r, c] - narrow[r] * narrow[c]
            for r, value in narrow.items():
                low[r, t] = jnp.concatenate([value, value], axis=1)
        solved = []
        for t in range(BLOCK):
            row = jnp.broadcast_to(rows[t : t + 1, :], (BLOCK, K))
            row = jnp.where(inside, jnp.where(lane == j + t, 1.0, 0.0), row)
            for s in range(t):
                row = row - low[t, s] * solved[s]
            solved.append(row * scale[t])
        if j + BLOCK < K:
            update = [None] * BLOCK
            for t in reversed(range(BLOCK)):
                row = solved[t]
                for s in range(t + 1, BLOCK):
                    row = row - low[s, t] * update[s]
                update[t] = row * scale[t]
            for i in range(j + BLOCK, K, BLOCK):
                below = work[i : i + BLOCK, :]
                new = jnp.where(inside, 0.0, below)
                for t in range(BLOCK):
                    new = new - jnp.broadcast_to(below[:, j + t : j + t + 1], (BLOCK, K)) * update[t]
                work[i : i + BLOCK, :] = new
        result = solved[0]
        for t in range(1, BLOCK):
            result = jnp.where(row_of == t, solved[t], result)
        out_ref[j : j + BLOCK, :] = jnp.where(lane < j + BLOCK, result, 0.0)


def inverse_factor(gram):
    return pl.pallas_call(
        inverse_factor_kernel,
        out_shape=jax.ShapeDtypeStruct((K, K), jnp.float32),
        in_specs=[pl.BlockSpec(memory_space=pltpu.VMEM)],
        out_specs=pl.BlockSpec(memory_space=pltpu.VMEM),
        scratch_shapes=[pltpu.VMEM((K, K), jnp.float32)],
        cost_estimate=pl.CostEstimate(flops=40_000_000, bytes_accessed=524_288, transcendentals=K),
    )(gram)


def swap(pieces, axis):
    return lax.all_to_all(pieces, axis, 0, 0, tiled=True)


def share(block, axis):
    return swap(jnp.broadcast_to(block[None], (lax.axis_size(axis),) + block.shape), axis)


def on_device(activations, sketch):
    tok_rows, panel = activations.shape
    half = panel // 2
    core = lax.axis_index("core")
    kept = lax.dynamic_slice_in_dim(activations, core * half, half, axis=1)
    given = lax.dynamic_slice_in_dim(activations, (1 - core) * half, half, axis=1)
    other = lax.ppermute(given, "core", [(0, 1), (1, 0)])

    with jax.named_scope("projected"):
        partial_sum = jnp.dot(activations, sketch, preferred_element_type=jnp.float32)
        summed = jnp.sum(swap(partial_sum.reshape(4, tok_rows // 4, K), "x"), axis=0)
        rows = (summed * (1.0 / math.sqrt(D))).astype(jnp.bfloat16)
        projected = share(rows, ("core", "x")).reshape(2, tok_rows, K)
        own = lax.dynamic_index_in_dim(projected, core, axis=0, keepdims=False)
        others = lax.dynamic_index_in_dim(projected, 1 - core, axis=0, keepdims=False)

    with jax.named_scope("moment"):
        over_tokens = (((0,), (0,)), ((), ()))
        chip_sum = lax.dot_general(
            kept, own, over_tokens, preferred_element_type=jnp.float32
        ) + lax.dot_general(other, others, over_tokens, preferred_element_type=jnp.float32)
        pieces = chip_sum.astype(jnp.bfloat16).reshape(8, half // 8, K)
        piece = jnp.sum(swap(pieces, "y").astype(jnp.float32), axis=0)
        part = jnp.sum(swap(piece.reshape(4, half // 32, K), "zl"), axis=0)
        part = jnp.sum(share(part, "zh"), axis=0)
        moment = share(part, "zl").reshape(half // 8, K) / TOKENS
        whole = lax.all_gather(moment, ("core", "y"), axis=0, tiled=True)

    with jax.named_scope("gram"):
        local_gram = lax.dot_general(
            moment, moment, over_tokens, precision=lax.Precision.HIGHEST
        )
        strip = jnp.sum(swap(local_gram.reshape(8, K // 8, K), ("core", "x")), axis=0)
        strip = jnp.sum(share(strip, "y"), axis=0)
        gram = share(strip, ("core", "x")).reshape(K, K)

    with jax.named_scope("new_basis"):
        inverse = inverse_factor(gram)
        solved = lax.dot_general(
            whole, inverse, (((1,), (1,)), ((), ())), precision=lax.Precision.HIGHEST
        )
        return (solved * math.sqrt(D)).astype(jnp.bfloat16)


def solution(mesh):
    fine = Mesh(mesh.devices.reshape(3, 4, 8, 2, 4), TOK + ("x",))
    return jax.shard_map(
        on_device,
        mesh=fine,
        in_specs=(P(TOK, "x"), P("x", None)),
        out_specs=P("x", None),
        check_vma=False,
    )
```

time: 1740 us -> 164 us (0.09)
  waiting for transfers between devices: 639 us -> 6.58 us
  starting transfers between devices: 582 us -> 23.8 us
  blocking collectives: 424 us -> 93.7 us
  other arithmetic: 55.3 us -> 0.82 us
    unnamed x60 -> x0, starting transfers between devices: 581 us -> none
    psum x2 -> x0, waiting for transfers between devices: 523 us -> none  [the longest x1 460 us: on_device(): gram = lax.psum(local_gram, ('tok', 'wid'))]
    unnamed x1 -> x0, blocking collectives: 424 us -> none
    all_gather x1, waiting for transfers between devices: 109 us -> 0.01 us  [on_device(): whole = lax.all_gather(moment, ('core', 'y'), axis=0, tiled=True)]
    all_to_all x0 -> x7, blocking collectives: none -> 93.7 us  [swap(): return lax.all_to_all(pieces, axis, 0, 0, tiled=True)]
    another operation x9 -> x0, other arithmetic: 53.7 us -> none  [the longest x6 34 us: on_device(): lower = jnp.linalg.cholesky(gram)]
  transfers between devices with their start and end apart: 63 -> 4, of which waited for: 5 -> 1; matrix products, arithmetic and copies ran while one was open for 0% -> 2% of each run, Pallas kernels for 0% -> 8%
where the time goes in v1:
time: 164 us
  blocking collectives  93.7 us (57%)
  starting transfers between devices  23.8 us (15%)
  between operations  13.5 us (8%)
  Pallas kernels  13.4 us (8%)
  matrix products  8.74 us (5%)
  waiting for transfers between devices  6.58 us (4%)
  local copies, waits for them, and re-layouts  3.03 us (2%)
    all_to_all x7, blocking collectives, swap(): return lax.all_to_all(pieces, axis, 0, 0, tiled=True)  93.7 us
    pallas_call x1, Pallas kernels, inverse_factor(): pl.pallas_call(inverse_factor_kernel, out_shape=jax.ShapeDtypeStruct((K,...  13.4 us
    all_to_all x2, starting transfers between devices, swap(): return lax.all_to_all(pieces, axis, 0, 0, tiled=True)  12.8 us
    ppermute x1, starting transfers between devices, on_device(): other = lax.ppermute(given, 'core', [(0, 1), (1, 0)])  11 us
    all_to_all x2, waiting for transfers between devices, swap(): return lax.all_to_all(pieces, axis, 0, 0, tiled=True)  6.56 us
    dot_general x1, matrix products, on_device(): lax.dot_general(whole, inverse, (((1,), (1,)), ((), ())), precision=lax.P...  4.4 us
  transfers between devices with their start and end apart: 4, of which 1 were waited for; matrix products, arithmetic and copies ran while one was open for 2% of the time, Pallas kernels for 8%

profile of v1, /device:TPU:1, one launch (start us, length us, event | category | flops | bytes accessed | tf_op | source)
XLA Modules:
  0.0 163.6 jit_solution(16884735247634163084)
XLA Ops:
  6.5 0.0 copy-start
  6.5 1.2 copy-done
  7.8 2.4 %fusion.10 = f32[256,256]{1,0:T(8,128)} fusion(bf16[256,2048]{1,0:T(8,128)(2,1)S(1)} %copy-done, bf16[2048,256]{1,0:T(8,128)(2,1)} %param.3), kind=kOutput, calls=%fused_computation.16 | convolution fusion | flops 268435456 | bytes 2359296 | tf_op jit(solution)/shard_map/projected/dot_general | solution.py:94
  10.1 4.8 %all-to-all-start = ((f32[4,64,256]{2,1,0:T(8,128)}), f32[4,64,256]{2,1,0:T(8,128)S(1)}, u32[]{:S(2)}, u32[]{:S(2)}) async-start(f32[4,64,256]{2,1,0:T(8,128)} %bitcast), calls=%async_computation | async-start | bytes 524288 | tf_op jit(solution)/shard_map/projected/all_to_all | solution.py:78
  15.0 11.0 %collective-permute-start = (bf16[256,1024]{1,0:T(8,128)(2,1)S(1)}, bf16[256,1024]{1,0:T(8,128)(2,1)S(1)}, u32[]{:S(2)}, u32[]{:S(2)}) collective-permute-start(bf16[256,1024]{1,0:T(8,128)(2,1)S(1)} %constant_dynamic-slice_fusion), channel_id=1, source_target_pairs={{0,4},{4,0},{1,5},{5,1},{2,6},{6,2},{3,7},{7,3},{8,12},{12,8},{9,1... | collective-permute-start | bytes 1572872 | tf_op jit(solution)/shard_map/ppermute | solution.py:91
  26.0 0.0 all-to-all-done
  26.1 0.7 broadcast_in_dim.10
  26.8 8.0 %all-to-all-start.1 = ((bf16[8,64,256]{2,1,0:T(8,128)(2,1)}), bf16[8,64,256]{2,1,0:T(8,128)(2,1)S(1)}, u32[]{:S(2)}, u32[]{:S(2)}) async-start(bf16[8,64,256]{2,1,0:T(8,128)(2,1)} %broadcast_in_dim.10), calls=%async_computation.1 | async-start | bytes 524288 | tf_op jit(solution)/shard_map/projected/all_to_all | solution.py:78
  34.8 0.0 all-gather.2.cloned.1.call-start
  34.8 6.6 %all-to-all-done.1 = bf16[8,64,256]{2,1,0:T(8,128)(2,1)S(1)} async-done(((bf16[8,64,256]{2,1,0:T(8,128)(2,1)}), bf16[8,64,256]{2,1,0:T(8,128)(2,1)S(1)}, u32[]{:S(2)}, u32[]{:S(2)}) %all-to-all-start.1) | async-done | bytes 262176 | tf_op jit(solution)/shard_map/projected/all_to_all | solution.py:78
  41.4 0.3 fusion.2
  41.7 0.0 collective-permute-done
  41.7 0.4 fusion.1
  42.1 20.4 %all_to_all.45 = bf16[8,128,256]{2,1,0:T(8,128)(2,1)S(1)} all-to-all(bf16[8,128,256]{2,1,0:T(8,128)(2,1)S(1)} %bitcast.24), channel_id=1, replica_groups=mesh['zh'=3,'zl'=4,'y'=8,'core'=2,'x'=4] {'y'}, dimensions={0} | all-to-all | bytes 1048576 | tf_op jit(solution)/shard_map/moment/all_to_all | solution.py:78
  62.5 0.1 convert_reduce_fusion
  62.5 7.3 %all_to_all.46 = f32[4,32,256]{2,1,0:T(8,128)S(1)} all-to-all(f32[4,32,256]{2,1,0:T(8,128)S(1)} %bitcast.31), channel_id=1, replica_groups=mesh['zh'=3,'zl'=4,'y'=8,'core'=2,'x'=4] {'zl'}, dimensions={0} | all-to-all | bytes 262144 | tf_op jit(solution)/shard_map/moment/all_to_all | solution.py:78
  69.8 16.9 %all_to_all.47 = f32[3,32,256]{2,1,0:T(8,128)S(1)} all-to-all(f32[3,32,256]{2,1,0:T(8,128)S(1)} %broadcast_in_dim.11), channel_id=1, replica_groups=mesh['zh'=3,'zl'=4,'y'=8,'core'=2,'x'=4] {'zh'}, dimensions={0} | all-to-all | bytes 196608 | tf_op jit(solution)/shard_map/moment/all_to_all | solution.py:78
  86.7 7.6 %all_to_all.48 = f32[4,32,256]{2,1,0:T(8,128)S(1)} all-to-all(f32[4,32,256]{2,1,0:T(8,128)S(1)} %broadcast_in_dim.12), channel_id=1, replica_groups=mesh['zh'=3,'zl'=4,'y'=8,'core'=2,'x'=4] {'zl'}, dimensions={0} | all-to-all | bytes 262144 | tf_op jit(solution)/shard_map/moment/all_to_all | solution.py:78
  94.3 0.7 broadcast_multiply_fusion
  95.0 0.0 all-gather.2.cloned.1.call-update
  95.0 1.0 copy.5
  96.0 1.3 fusion.11
  97.3 14.5 %all_to_all.49 = f32[8,32,256]{2,1,0:T(8,128)S(1)} all-to-all(f32[8,32,256]{2,1,0:T(8,128)S(1)} %fusion.11), channel_id=1, replica_groups=mesh['zh'=3,'zl'=4,'y'=8,'core'=2,'x'=4] {'core','x'}, dimensions={0} | all-to-all | bytes 524288 | tf_op jit(solution)/shard_map/gram/all_to_all | solution.py:78
  111.8 16.8 %all_to_all.50 = f32[8,32,256]{2,1,0:T(8,128)S(1)} all-to-all(f32[8,32,256]{2,1,0:T(8,128)S(1)} %broadcast_in_dim.13), channel_id=1, replica_groups=mesh['zh'=3,'zl'=4,'y'=8,'core'=2,'x'=4] {'y'}, dimensions={0} | all-to-all | bytes 524288 | tf_op jit(solution)/shard_map/gram/all_to_all | solution.py:78
  128.6 10.4 %all_to_all.51 = f32[8,32,256]{2,1,0:T(8,128)} all-to-all(f32[8,32,256]{2,1,0:T(8,128)S(1)} %broadcast_in_dim.14), channel_id=1, replica_groups=mesh['zh'=3,'zl'=4,'y'=8,'core'=2,'x'=4] {'core','x'}, dimensions={0} | all-to-all | bytes 524288 | tf_op jit(solution)/shard_map/gram/all_to_all | solution.py:78
  139.0 13.4 %new_basis.1 = f32[256,256]{1,0:T(8,128)} custom-call(f32[256,256]{1,0:T(8,128)} %bitcast.30), custom_call_target="tpu_custom_call" | custom-call | flops 40000000 | bytes 524288 | tf_op jit(solution)/shard_map/new_basis/pallas_call | solution.py:67
  152.4 0.0 all-gather.2.cloned.1.call-done
  152.4 4.4 %fusion = bf16[2048,256]{1,0:T(8,128)(2,1)} fusion(f32[2048,256]{1,0:T(8,128)} %all-gather.2.cloned.1.call-done, f32[256,256]{1,0:T(8,128)} %new_basis.1), kind=kOutput, calls=%fused_computation.1 | convolution fusion | flops 1611661312 | bytes 3407872 | tf_op jit(solution)/shard_map/new_basis/dot_general | solution.py:123
  (11 shorter events, 0.2 us)
Async XLA Ops:
  6.5 1.2 copy-start
  10.1 15.9 %all-to-all-start = ((f32[4,64,256]{2,1,0:T(8,128)}), f32[4,64,256]{2,1,0:T(8,128)S(1)}, u32[]{:S(2)}, u32[]{:S(2)}) async-start(f32[4,64,256]{2,1,0:T(8,128)} %bitcast), calls=%async_computation | async-start | bytes 524288 | tf_op jit(solution)/shard_map/projected/all_to_all | solution.py:78
  15.0 26.7 %collective-permute-start = (bf16[256,1024]{1,0:T(8,128)(2,1)S(1)}, bf16[256,1024]{1,0:T(8,128)(2,1)S(1)}, u32[]{:S(2)}, u32[]{:S(2)}) collective-permute-start(bf16[256,1024]{1,0:T(8,128)(2,1)S(1)} %constant_dynamic-slice_fusion), channel_id=1, source_target_pairs={{0,4},{4,0},{1,5},{5,1},{2,6},{6,2},{3,7},{7,3},{8,12},{12,8},{9,1... | collective-permute-start | bytes 1572872 | tf_op jit(solution)/shard_map/ppermute | solution.py:91
  26.8 14.6 %all-to-all-start.1 = ((bf16[8,64,256]{2,1,0:T(8,128)(2,1)}), bf16[8,64,256]{2,1,0:T(8,128)(2,1)S(1)}, u32[]{:S(2)}, u32[]{:S(2)}) async-start(bf16[8,64,256]{2,1,0:T(8,128)(2,1)} %broadcast_in_dim.10), calls=%async_computation.1 | async-start | bytes 524288 | tf_op jit(solution)/shard_map/projected/all_to_all | solution.py:78
  34.8 117.6 %all-gather.2.cloned.1.call-start = ((), (), s32[]{:S(2)}) async-start(), calls=%async_computation.9 | async-start | bytes 2228224 | tf_op jit(solution)/shard_map/moment/all_gather | solution.py:111
Sparse Core Ops, SparseCore 0:
  95.1 42.3 all-gather.1

commit v2 on v1

--- a/solution.py
+++ b/solution.py
@@ -18,40 +18,57 @@
     work[...] = gram_ref[...]
     lane = lax.broadcasted_iota(jnp.int32, (BLOCK, K), 1)
     row_of = lax.broadcasted_iota(jnp.int32, (BLOCK, K), 0)
+
+    def wide(value):
+        return jnp.concatenate([value, value], axis=1)
+
+    def column(block, k):
+        return jnp.broadcast_to(block[:, k : k + 1], (BLOCK, 128))
+
     for j in range(0, K, BLOCK):
         inside = (lane >= j) & (lane < j + BLOCK)
         rows = work[j : j + BLOCK, :]
-        columns = [jnp.broadcast_to(rows[:, j + c : j + c + 1], (BLOCK, 128)) for c in range(BLOCK)]
+        columns = [column(rows, j + c) for c in range(BLOCK)]
         left = {
             (r, c): jnp.broadcast_to(columns[c][r : r + 1, :], (BLOCK, 128))
             for c in range(BLOCK)
             for r in range(c, BLOCK)
         }
-        scale, low = [], {}
+        near = j + BLOCK if j + BLOCK < K else None
+        if near is not None:
+            below = work[near : near + BLOCK, :]
+            below_columns = [column(below, j + c) for c in range(BLOCK)]
+            new = jnp.where(inside, 0.0, below)
+        scale, low, solved = [], {}, []
         for t in range(BLOCK):
             inv = lax.rsqrt(left[t, t])
-            scale.append(jnp.concatenate([inv, inv], axis=1))
             narrow = {r: left[r, t] * inv for r in range(t + 1, BLOCK)}
             for c in range(t + 1, BLOCK):
                 for r in range(c, BLOCK):
                     left[r, c] = left[r, c] - narrow[r] * narrow[c]
             for r, value in narrow.items():
-                low[r, t] = jnp.concatenate([value, value], axis=1)
-        solved = []
-        for t in range(BLOCK):
+                low[r, t] = wide(value)
+            scale.append(wide(inv))
             row = jnp.broadcast_to(rows[t : t + 1, :], (BLOCK, K))
             row = jnp.where(inside, jnp.where(lane == j + t, 1.0, 0.0), row)
             for s in range(t):
                 row = row - low[t, s] * solved[s]
             solved.append(row * scale[t])
-        if j + BLOCK < K:
+            if near is not None:
+                factor = below_columns[t] * inv
+                for c in range(t + 1, BLOCK):
+                    below_columns[c] = below_columns[c] - factor * narrow[c]
+                new = new - wide(factor) * solved[t]
+        if near is not None:
+            work[near : near + BLOCK, :] = new
+        if j + 2 * BLOCK < K:
             update = [None] * BLOCK
             for t in reversed(range(BLOCK)):
                 row = solved[t]
                 for s in range(t + 1, BLOCK):
                     row = row - low[s, t] * update[s]
                 update[t] = row * scale[t]
-            for i in range(j + BLOCK, K, BLOCK):
+            for i in range(j + 2 * BLOCK, K, BLOCK):
                 below = work[i : i + BLOCK, :]
                 new = jnp.where(inside, 0.0, below)
                 for t in range(BLOCK):
@@ -103,25 +120,24 @@
         chip_sum = lax.dot_general(
             kept, own, over_tokens, preferred_element_type=jnp.float32
         ) + lax.dot_general(other, others, over_tokens, preferred_element_type=jnp.float32)
-        pieces = chip_sum.astype(jnp.bfloat16).reshape(8, half // 8, K)
-        piece = jnp.sum(swap(pieces, "y").astype(jnp.float32), axis=0)
-        part = jnp.sum(swap(piece.reshape(4, half // 32, K), "zl"), axis=0)
+        pieces = chip_sum.astype(jnp.bfloat16).reshape(32, half // 32, K)
+        part = jnp.sum(swap(pieces, ("y", "zl")).astype(jnp.float32), axis=0)
         part = jnp.sum(share(part, "zh"), axis=0)
-        moment = share(part, "zl").reshape(half // 8, K) / TOKENS
-        whole = lax.all_gather(moment, ("core", "y"), axis=0, tiled=True)
+        moment = part / TOKENS
+        whole = lax.all_gather(moment, ("core", "y", "zl"), axis=0, tiled=True)
 
     with jax.named_scope("gram"):
         local_gram = lax.dot_general(
             moment, moment, over_tokens, precision=lax.Precision.HIGHEST
         )
-        strip = jnp.sum(swap(local_gram.reshape(8, K // 8, K), ("core", "x")), axis=0)
+        strip = jnp.sum(swap(local_gram.reshape(32, K // 32, K), ("zl", "core", "x")), axis=0)
         strip = jnp.sum(share(strip, "y"), axis=0)
-        gram = share(strip, ("core", "x")).reshape(K, K)
+        gram = share(strip, ("zl", "core", "x")).reshape(K, K)
 
     with jax.named_scope("new_basis"):
         inverse = inverse_factor(gram)
         solved = lax.dot_general(
-            whole, inverse, (((1,), (1,)), ((), ())), precision=lax.Precision.HIGHEST
+            whole, inverse, (((1,), (1,)), ((), ())), precision=lax.Precision.HIGH
         )
         return (solved * math.sqrt(D)).astype(jnp.bfloat16)
 

time: 164 us -> 208 us (1.27)
  waiting for transfers between devices: 6.58 us -> 63.1 us
  blocking collectives: 93.7 us -> 85.5 us
    all_gather x1, waiting for transfers between devices: 0.01 us -> 56.5 us  [on_device(): whole = lax.all_gather(moment, ('core', 'y', 'zl'), axis=0, tiled=True)]
    all_to_all x7 -> x5, blocking collectives: 93.7 us -> 85.5 us  [swap(): return lax.all_to_all(pieces, axis, 0, 0, tiled=True)]
  transfers between devices with their start and end apart: 4 -> 4, of which waited for: 1 -> 2; matrix products, arithmetic and copies ran while one was open for 2% -> 1% of each run, Pallas kernels for 8% -> 6%
where the time goes in v2:
time: 208 us
  blocking collectives  85.5 us (41%)
  waiting for transfers between devices  63.1 us (30%)
  starting transfers between devices  23.8 us (11%)
  between operations  13.5 us (6%)
  Pallas kernels  12.1 us (6%)
  matrix products  7.08 us (3%)
    all_to_all x5, blocking collectives, swap(): return lax.all_to_all(pieces, axis, 0, 0, tiled=True)  85.5 us
    all_gather x1, waiting for transfers between devices, on_device(): whole = lax.all_gather(moment, ('core', 'y', 'zl'), axis=0, tiled=True)  56.5 us
    all_to_all x2, starting transfers between devices, swap(): return lax.all_to_all(pieces, axis, 0, 0, tiled=True)  12.8 us
    pallas_call x1, Pallas kernels, inverse_factor(): pl.pallas_call(inverse_factor_kernel, out_shape=jax.ShapeDtypeStruct((K,...  12.1 us
    ppermute x1, starting transfers between devices, on_device(): other = lax.ppermute(given, 'core', [(0, 1), (1, 0)])  11 us
    all_to_all x2, waiting for transfers between devices, swap(): return lax.all_to_all(pieces, axis, 0, 0, tiled=True)  6.56 us
  transfers between devices with their start and end apart: 4, of which 2 were waited for; matrix products, arithmetic and copies ran while one was open for 1% of the time, Pallas kernels for 6%

profile of v2, /device:TPU:1, one launch (start us, length us, event | category | flops | bytes accessed | tf_op | source)
XLA Modules:
  0.0 207.8 jit_solution(4389367178561876989)
XLA Ops:
  6.5 0.0 copy-start
  6.5 1.2 copy-done
  7.8 2.4 %fusion.10 = f32[256,256]{1,0:T(8,128)} fusion(bf16[256,2048]{1,0:T(8,128)(2,1)S(1)} %copy-done, bf16[2048,256]{1,0:T(8,128)(2,1)} %param.3), kind=kOutput, calls=%fused_computation.17 | convolution fusion | flops 268435456 | bytes 2359296 | tf_op jit(solution)/shard_map/projected/dot_general | solution.py:111
  10.1 4.8 %all-to-all-start = ((f32[4,64,256]{2,1,0:T(8,128)}), f32[4,64,256]{2,1,0:T(8,128)S(1)}, u32[]{:S(2)}, u32[]{:S(2)}) async-start(f32[4,64,256]{2,1,0:T(8,128)} %bitcast), calls=%async_computation | async-start | bytes 524288 | tf_op jit(solution)/shard_map/projected/all_to_all | solution.py:95
  15.0 11.0 %collective-permute-start = (bf16[256,1024]{1,0:T(8,128)(2,1)S(1)}, bf16[256,1024]{1,0:T(8,128)(2,1)S(1)}, u32[]{:S(2)}, u32[]{:S(2)}) collective-permute-start(bf16[256,1024]{1,0:T(8,128)(2,1)S(1)} %constant_dynamic-slice_fusion), channel_id=1, source_target_pairs={{0,4},{4,0},{1,5},{5,1},{2,6},{6,2},{3,7},{7,3},{8,12},{12,8},{9,1... | collective-permute-start | bytes 1572872 | tf_op jit(solution)/shard_map/ppermute | solution.py:108
  26.0 0.0 all-to-all-done
  26.1 0.7 broadcast_in_dim.8
  26.8 8.0 %all-to-all-start.1 = ((bf16[8,64,256]{2,1,0:T(8,128)(2,1)}), bf16[8,64,256]{2,1,0:T(8,128)(2,1)S(1)}, u32[]{:S(2)}, u32[]{:S(2)}) async-start(bf16[8,64,256]{2,1,0:T(8,128)(2,1)} %broadcast_in_dim.8), calls=%async_computation.1 | async-start | bytes 524288 | tf_op jit(solution)/shard_map/projected/all_to_all | solution.py:95
  34.8 0.0 all-gather.2.cloned.1.call-start
  34.8 6.6 %all-to-all-done.1 = bf16[8,64,256]{2,1,0:T(8,128)(2,1)S(1)} async-done(((bf16[8,64,256]{2,1,0:T(8,128)(2,1)}), bf16[8,64,256]{2,1,0:T(8,128)(2,1)S(1)}, u32[]{:S(2)}, u32[]{:S(2)}) %all-to-all-start.1) | async-done | bytes 262176 | tf_op jit(solution)/shard_map/projected/all_to_all | solution.py:95
  41.4 0.3 fusion.2
  41.7 0.0 collective-permute-done
  41.7 0.4 fusion.1
  42.1 19.7 %all_to_all.35 = bf16[32,32,256]{2,1,0:T(8,128)(2,1)S(1)} all-to-all(bf16[32,32,256]{2,1,0:T(8,128)(2,1)S(1)} %bitcast.17), channel_id=1, replica_groups=mesh['zh'=3,'zl'=4,'y'=8,'core'=2,'x'=4] {'y','zl'}, dimensions={0} | all-to-all | bytes 1048576 | tf_op jit(solution)/shard_map/moment/all_to_all | solution.py:95
  61.8 0.1 convert_reduce_fusion
  61.9 17.6 %all_to_all.36 = f32[3,32,256]{2,1,0:T(8,128)S(1)} all-to-all(f32[3,32,256]{2,1,0:T(8,128)S(1)} %broadcast_in_dim.9), channel_id=1, replica_groups=mesh['zh'=3,'zl'=4,'y'=8,'core'=2,'x'=4] {'zh'}, dimensions={0} | all-to-all | bytes 196608 | tf_op jit(solution)/shard_map/moment/all_to_all | solution.py:95
  79.5 0.6 broadcast_multiply_fusion
  80.1 0.0 all-gather.2.cloned.1.call-update
  80.1 0.4 convolution_bitcast_fusion
  80.6 21.5 %all_to_all.37 = f32[32,8,256]{2,1,0:T(8,128)S(1)} all-to-all(f32[32,8,256]{2,1,0:T(8,128)S(1)} %convolution_bitcast_fusion), channel_id=1, replica_groups=mesh['zh'=3,'zl'=4,'y'=8,'core'=2,'x'=4] {'zl','core','x'}, dimensions={0} | all-to-all | bytes 524288 | tf_op jit(solution)/shard_map/gram/all_to_all | solution.py:95
  102.1 9.5 %all_to_all.38 = f32[8,8,256]{2,1,0:T(8,128)S(1)} all-to-all(f32[8,8,256]{2,1,0:T(8,128)S(1)} %broadcast_in_dim.10), channel_id=1, replica_groups=mesh['zh'=3,'zl'=4,'y'=8,'core'=2,'x'=4] {'y'}, dimensions={0} | all-to-all | bytes 131072 | tf_op jit(solution)/shard_map/gram/all_to_all | solution.py:95
  111.7 17.1 %all_to_all.39 = f32[32,8,256]{2,1,0:T(8,128)} all-to-all(f32[32,8,256]{2,1,0:T(8,128)S(1)} %broadcast_in_dim.11), channel_id=1, replica_groups=mesh['zh'=3,'zl'=4,'y'=8,'core'=2,'x'=4] {'zl','core','x'}, dimensions={0} | all-to-all | bytes 524288 | tf_op jit(solution)/shard_map/gram/all_to_all | solution.py:95
  128.8 12.1 %new_basis.1 = f32[256,256]{1,0:T(8,128)} custom-call(f32[256,256]{1,0:T(8,128)} %bitcast.20), custom_call_target="tpu_custom_call" | custom-call | flops 40000000 | bytes 524288 | tf_op jit(solution)/shard_map/new_basis/pallas_call | solution.py:84
  140.9 56.5 %all-gather.2.cloned.1.call-done = f32[2048,256]{1,0:T(8,128)} async-done(((f32[32,256]{1,0:T(8,128)}), f32[2048,256]{1,0:T(8,128)}) %all-gather.2.cloned.1.call-update) | async-done | bytes 2097168 | tf_op jit(solution)/shard_map/moment/all_gather | solution.py:127
  197.4 3.6 %fusion = bf16[2048,256]{1,0:T(8,128)(2,1)} fusion(f32[2048,256]{1,0:T(8,128)} %all-gather.2.cloned.1.call-done, f32[256,256]{1,0:T(8,128)} %new_basis.1), kind=kOutput, calls=%fused_computation.1 | convolution fusion | flops 806354944 | bytes 3407872 | tf_op jit(solution)/shard_map/new_basis/dot_general | solution.py:139
  (9 shorter events, 0.2 us)
Async XLA Ops:
  6.5 1.2 copy-start
  10.1 15.9 %all-to-all-start = ((f32[4,64,256]{2,1,0:T(8,128)}), f32[4,64,256]{2,1,0:T(8,128)S(1)}, u32[]{:S(2)}, u32[]{:S(2)}) async-start(f32[4,64,256]{2,1,0:T(8,128)} %bitcast), calls=%async_computation | async-start | bytes 524288 | tf_op jit(solution)/shard_map/projected/all_to_all | solution.py:95
  15.0 26.7 %collective-permute-start = (bf16[256,1024]{1,0:T(8,128)(2,1)S(1)}, bf16[256,1024]{1,0:T(8,128)(2,1)S(1)}, u32[]{:S(2)}, u32[]{:S(2)}) collective-permute-start(bf16[256,1024]{1,0:T(8,128)(2,1)S(1)} %constant_dynamic-slice_fusion), channel_id=1, source_target_pairs={{0,4},{4,0},{1,5},{5,1},{2,6},{6,2},{3,7},{7,3},{8,12},{12,8},{9,1... | collective-permute-start | bytes 1572872 | tf_op jit(solution)/shard_map/ppermute | solution.py:108
  26.8 14.6 %all-to-all-start.1 = ((bf16[8,64,256]{2,1,0:T(8,128)(2,1)}), bf16[8,64,256]{2,1,0:T(8,128)(2,1)S(1)}, u32[]{:S(2)}, u32[]{:S(2)}) async-start(bf16[8,64,256]{2,1,0:T(8,128)(2,1)} %broadcast_in_dim.8), calls=%async_computation.1 | async-start | bytes 524288 | tf_op jit(solution)/shard_map/projected/all_to_all | solution.py:95
  34.8 162.6 %all-gather.2.cloned.1.call-start = ((), (), s32[]{:S(2)}) async-start(), calls=%async_computation.7 | async-start | bytes 2129920 | tf_op jit(solution)/shard_map/moment/all_gather | solution.py:127
Sparse Core Ops, SparseCore 0:
  80.3 117.0 all-gather.1

commit v3 on v2

--- a/solution.py
+++ b/solution.py
@@ -123,14 +123,17 @@
         pieces = chip_sum.astype(jnp.bfloat16).reshape(32, half // 32, K)
         part = jnp.sum(swap(pieces, ("y", "zl")).astype(jnp.float32), axis=0)
         part = jnp.sum(share(part, "zh"), axis=0)
-        moment = part / TOKENS
-        whole = lax.all_gather(moment, ("core", "y", "zl"), axis=0, tiled=True)
+        moment = share(part, "zl").reshape(half // 8, K) / TOKENS
+        whole = lax.all_gather(moment, ("core", "y"), axis=0, tiled=True)
 
     with jax.named_scope("gram"):
         local_gram = lax.dot_general(
             moment, moment, over_tokens, precision=lax.Precision.HIGHEST
         )
-        strip = jnp.sum(swap(local_gram.reshape(32, K // 32, K), ("zl", "core", "x")), axis=0)
+        quarter = lax.dynamic_slice_in_dim(
+            local_gram, lax.axis_index("zl") * (K // 4), K // 4, axis=0
+        )
+        strip = jnp.sum(swap(quarter.reshape(8, K // 32, K), ("core", "x")), axis=0)
         strip = jnp.sum(share(strip, "y"), axis=0)
         gram = share(strip, ("zl", "core", "x")).reshape(K, K)
 

time: 208 us -> 153 us (0.74)
  waiting for transfers between devices: 63.1 us -> 6.58 us
    all_gather x1, waiting for transfers between devices: 56.5 us -> 0.01 us  [on_device(): whole = lax.all_gather(moment, ('core', 'y'), axis=0, tiled=True)]
    all_to_all x5 -> x6, blocking collectives: 85.5 us -> 86.1 us  [swap(): return lax.all_to_all(pieces, axis, 0, 0, tiled=True)]
  transfers between devices with their start and end apart: 4 -> 4, of which waited for: 2 -> 1; matrix products, arithmetic and copies ran while one was open for 1% -> 1% of each run, Pallas kernels for 6% -> 8%
where the time goes in v3:
time: 153 us; the launch traced here: 152 us
  blocking collectives  86.1 us (56%)
  starting transfers between devices  23.8 us (16%)
  between operations  13.5 us (9%)
  Pallas kernels  12.1 us (8%)
  matrix products  7.08 us (5%)
  waiting for transfers between devices  6.58 us (4%)
  local copies, waits for them, and re-layouts  2.04 us (1%)
    all_to_all x6, blocking collectives, swap(): return lax.all_to_all(pieces, axis, 0, 0, tiled=True)  86.1 us
    all_to_all x2, starting transfers between devices, swap(): return lax.all_to_all(pieces, axis, 0, 0, tiled=True)  12.8 us
    pallas_call x1, Pallas kernels, inverse_factor(): pl.pallas_call(inverse_factor_kernel, out_shape=jax.ShapeDtypeStruct((K,...  12.1 us
    ppermute x1, starting transfers between devices, on_device(): other = lax.ppermute(given, 'core', [(0, 1), (1, 0)])  11 us
    all_to_all x2, waiting for transfers between devices, swap(): return lax.all_to_all(pieces, axis, 0, 0, tiled=True)  6.56 us
    dot_general x1, matrix products, on_device(): lax.dot_general(whole, inverse, (((1,), (1,)), ((), ())), precision=lax.P...  3.6 us
  transfers between devices with their start and end apart: 4, of which 1 were waited for; matrix products, arithmetic and copies ran while one was open for 1% of the time, Pallas kernels for 8%

profile of v3, /device:TPU:1, one launch (start us, length us, event | category | flops | bytes accessed | tf_op | source)
XLA Modules:
  0.0 152.0 jit_solution(12922656379733955526)
XLA Ops:
  6.5 0.0 copy-start
  6.5 1.2 copy-done
  7.8 2.4 %fusion.10 = f32[256,256]{1,0:T(8,128)} fusion(bf16[256,2048]{1,0:T(8,128)(2,1)S(1)} %copy-done, bf16[2048,256]{1,0:T(8,128)(2,1)} %param.3), kind=kOutput, calls=%fused_computation.18 | convolution fusion | flops 268435456 | bytes 2359296 | tf_op jit(solution)/shard_map/projected/dot_general | solution.py:111
  10.1 4.8 %all-to-all-start = ((f32[4,64,256]{2,1,0:T(8,128)}), f32[4,64,256]{2,1,0:T(8,128)S(1)}, u32[]{:S(2)}, u32[]{:S(2)}) async-start(f32[4,64,256]{2,1,0:T(8,128)} %bitcast), calls=%async_computation | async-start | bytes 524288 | tf_op jit(solution)/shard_map/projected/all_to_all | solution.py:95
  15.0 11.0 %collective-permute-start = (bf16[256,1024]{1,0:T(8,128)(2,1)S(1)}, bf16[256,1024]{1,0:T(8,128)(2,1)S(1)}, u32[]{:S(2)}, u32[]{:S(2)}) collective-permute-start(bf16[256,1024]{1,0:T(8,128)(2,1)S(1)} %constant_dynamic-slice_fusion), channel_id=1, source_target_pairs={{0,4},{4,0},{1,5},{5,1},{2,6},{6,2},{3,7},{7,3},{8,12},{12,8},{9,1... | collective-permute-start | bytes 1572872 | tf_op jit(solution)/shard_map/ppermute | solution.py:108
  26.0 0.0 all-to-all-done
  26.1 0.7 broadcast_in_dim.10
  26.8 8.0 %all-to-all-start.1 = ((bf16[8,64,256]{2,1,0:T(8,128)(2,1)}), bf16[8,64,256]{2,1,0:T(8,128)(2,1)S(1)}, u32[]{:S(2)}, u32[]{:S(2)}) async-start(bf16[8,64,256]{2,1,0:T(8,128)(2,1)} %broadcast_in_dim.10), calls=%async_computation.1 | async-start | bytes 524288 | tf_op jit(solution)/shard_map/projected/all_to_all | solution.py:95
  34.8 0.0 all-gather.2.cloned.1.call-start
  34.8 6.6 %all-to-all-done.1 = bf16[8,64,256]{2,1,0:T(8,128)(2,1)S(1)} async-done(((bf16[8,64,256]{2,1,0:T(8,128)(2,1)}), bf16[8,64,256]{2,1,0:T(8,128)(2,1)S(1)}, u32[]{:S(2)}, u32[]{:S(2)}) %all-to-all-start.1) | async-done | bytes 262176 | tf_op jit(solution)/shard_map/projected/all_to_all | solution.py:95
  41.4 0.3 fusion.2
  41.7 0.0 collective-permute-done
  41.7 0.4 fusion.1
  42.1 19.7 %all_to_all.40 = bf16[32,32,256]{2,1,0:T(8,128)(2,1)S(1)} all-to-all(bf16[32,32,256]{2,1,0:T(8,128)(2,1)S(1)} %bitcast.20), channel_id=1, replica_groups=mesh['zh'=3,'zl'=4,'y'=8,'core'=2,'x'=4] {'y','zl'}, dimensions={0} | all-to-all | bytes 1048576 | tf_op jit(solution)/shard_map/moment/all_to_all | solution.py:95
  61.8 0.1 convert_reduce_fusion
  61.9 17.6 %all_to_all.41 = f32[3,32,256]{2,1,0:T(8,128)S(1)} all-to-all(f32[3,32,256]{2,1,0:T(8,128)S(1)} %broadcast_in_dim.11), channel_id=1, replica_groups=mesh['zh'=3,'zl'=4,'y'=8,'core'=2,'x'=4] {'zh'}, dimensions={0} | all-to-all | bytes 196608 | tf_op jit(solution)/shard_map/moment/all_to_all | solution.py:95
  79.5 9.8 %all_to_all.42 = f32[4,32,256]{2,1,0:T(8,128)S(1)} all-to-all(f32[4,32,256]{2,1,0:T(8,128)S(1)} %broadcast_in_dim.12), channel_id=1, replica_groups=mesh['zh'=3,'zl'=4,'y'=8,'core'=2,'x'=4] {'zl'}, dimensions={0} | all-to-all | bytes 262144 | tf_op jit(solution)/shard_map/moment/all_to_all | solution.py:95
  89.3 0.7 broadcast_multiply_fusion
  90.0 0.0 all-gather.2.cloned.1.call-update
  90.0 0.4 convolution_bitcast_fusion
  90.5 12.5 %all_to_all.43 = f32[8,8,256]{2,1,0:T(8,128)S(1)} all-to-all(f32[8,8,256]{2,1,0:T(8,128)S(1)} %dynamic-slice_bitcast_fusion), channel_id=1, replica_groups=mesh['zh'=3,'zl'=4,'y'=8,'core'=2,'x'=4] {'core','x'}, dimensions={0} | all-to-all | bytes 131072 | tf_op jit(solution)/shard_map/gram/all_to_all | solution.py:95
  103.0 9.5 %all_to_all.44 = f32[8,8,256]{2,1,0:T(8,128)S(1)} all-to-all(f32[8,8,256]{2,1,0:T(8,128)S(1)} %broadcast_in_dim.13), channel_id=1, replica_groups=mesh['zh'=3,'zl'=4,'y'=8,'core'=2,'x'=4] {'y'}, dimensions={0} | all-to-all | bytes 131072 | tf_op jit(solution)/shard_map/gram/all_to_all | solution.py:95
  112.5 17.0 %all_to_all.45 = f32[32,8,256]{2,1,0:T(8,128)} all-to-all(f32[32,8,256]{2,1,0:T(8,128)S(1)} %broadcast_in_dim.14), channel_id=1, replica_groups=mesh['zh'=3,'zl'=4,'y'=8,'core'=2,'x'=4] {'zl','core','x'}, dimensions={0} | all-to-all | bytes 524288 | tf_op jit(solution)/shard_map/gram/all_to_all | solution.py:95
  129.5 12.1 %new_basis.1 = f32[256,256]{1,0:T(8,128)} custom-call(f32[256,256]{1,0:T(8,128)} %bitcast.23), custom_call_target="tpu_custom_call" | custom-call | flops 40000000 | bytes 524288 | tf_op jit(solution)/shard_map/new_basis/pallas_call | solution.py:84
  141.6 0.0 all-gather.2.cloned.1.call-done
  141.6 3.6 %fusion = bf16[2048,256]{1,0:T(8,128)(2,1)} fusion(f32[2048,256]{1,0:T(8,128)} %all-gather.2.cloned.1.call-done, f32[256,256]{1,0:T(8,128)} %new_basis.1), kind=kOutput, calls=%fused_computation.1 | convolution fusion | flops 806354944 | bytes 3407872 | tf_op jit(solution)/shard_map/new_basis/dot_general | solution.py:142
  (11 shorter events, 0.2 us)
Async XLA Ops:
  6.5 1.2 copy-start
  10.1 15.9 %all-to-all-start = ((f32[4,64,256]{2,1,0:T(8,128)}), f32[4,64,256]{2,1,0:T(8,128)S(1)}, u32[]{:S(2)}, u32[]{:S(2)}) async-start(f32[4,64,256]{2,1,0:T(8,128)} %bitcast), calls=%async_computation | async-start | bytes 524288 | tf_op jit(solution)/shard_map/projected/all_to_all | solution.py:95
  15.0 26.7 %collective-permute-start = (bf16[256,1024]{1,0:T(8,128)(2,1)S(1)}, bf16[256,1024]{1,0:T(8,128)(2,1)S(1)}, u32[]{:S(2)}, u32[]{:S(2)}) collective-permute-start(bf16[256,1024]{1,0:T(8,128)(2,1)S(1)} %constant_dynamic-slice_fusion), channel_id=1, source_target_pairs={{0,4},{4,0},{1,5},{5,1},{2,6},{6,2},{3,7},{7,3},{8,12},{12,8},{9,1... | collective-permute-start | bytes 1572872 | tf_op jit(solution)/shard_map/ppermute | solution.py:108
  26.8 14.5 %all-to-all-start.1 = ((bf16[8,64,256]{2,1,0:T(8,128)(2,1)}), bf16[8,64,256]{2,1,0:T(8,128)(2,1)S(1)}, u32[]{:S(2)}, u32[]{:S(2)}) async-start(bf16[8,64,256]{2,1,0:T(8,128)(2,1)} %broadcast_in_dim.10), calls=%async_computation.1 | async-start | bytes 524288 | tf_op jit(solution)/shard_map/projected/all_to_all | solution.py:95
  34.8 106.8 %all-gather.2.cloned.1.call-start = ((), (), s32[]{:S(2)}) async-start(), calls=%async_computation.8 | async-start | bytes 2228224 | tf_op jit(solution)/shard_map/moment/all_gather | solution.py:127
Sparse Core Ops, SparseCore 0:
  90.1 39.4 all-gather.1

commit v4 on v3

--- a/solution.py
+++ b/solution.py
@@ -11,7 +11,7 @@
 K = 256
 TOKENS = 49152
 BLOCK = 8
-TOK = ("zh", "zl", "y", "core")
+TOK = ("zh", "zm", "zl", "y", "core")
 
 
 def inverse_factor_kernel(gram_ref, out_ref, work):
@@ -109,11 +109,9 @@
 
     with jax.named_scope("projected"):
         partial_sum = jnp.dot(activations, sketch, preferred_element_type=jnp.float32)
-        summed = jnp.sum(swap(partial_sum.reshape(4, tok_rows // 4, K), "x"), axis=0)
-        rows = (summed * (1.0 / math.sqrt(D))).astype(jnp.bfloat16)
-        projected = share(rows, ("core", "x")).reshape(2, tok_rows, K)
-        own = lax.dynamic_index_in_dim(projected, core, axis=0, keepdims=False)
-        others = lax.dynamic_index_in_dim(projected, 1 - core, axis=0, keepdims=False)
+        terms = share(partial_sum.astype(jnp.bfloat16), "x").astype(jnp.float32)
+        own = (jnp.sum(terms, axis=0) * (1.0 / math.sqrt(D))).astype(jnp.bfloat16)
+        others = lax.ppermute(own, "core", [(0, 1), (1, 0)])
 
     with jax.named_scope("moment"):
         over_tokens = (((0,), (0,)), ((), ()))
@@ -121,19 +119,19 @@
             kept, own, over_tokens, preferred_element_type=jnp.float32
         ) + lax.dot_general(other, others, over_tokens, preferred_element_type=jnp.float32)
         pieces = chip_sum.astype(jnp.bfloat16).reshape(32, half // 32, K)
-        part = jnp.sum(swap(pieces, ("y", "zl")).astype(jnp.float32), axis=0)
+        part = jnp.sum(swap(pieces, ("y", "zm", "zl")).astype(jnp.float32), axis=0)
         part = jnp.sum(share(part, "zh"), axis=0)
-        moment = share(part, "zl").reshape(half // 8, K) / TOKENS
+        moment = share(part, ("zm", "zl")).reshape(half // 8, K) / TOKENS
         whole = lax.all_gather(moment, ("core", "y"), axis=0, tiled=True)
 
     with jax.named_scope("gram"):
         local_gram = lax.dot_general(
             moment, moment, over_tokens, precision=lax.Precision.HIGHEST
         )
-        quarter = lax.dynamic_slice_in_dim(
-            local_gram, lax.axis_index("zl") * (K // 4), K // 4, axis=0
+        part_gram = lax.dynamic_slice_in_dim(
+            local_gram, lax.axis_index("zl") * (K // 2), K // 2, axis=0
         )
-        strip = jnp.sum(swap(quarter.reshape(8, K // 32, K), ("core", "x")), axis=0)
+        strip = jnp.sum(swap(part_gram.reshape(8, K // 16, K), ("core", "x")), axis=0)
         strip = jnp.sum(share(strip, "y"), axis=0)
         gram = share(strip, ("zl", "core", "x")).reshape(K, K)
 
@@ -146,7 +144,7 @@
 
 
 def solution(mesh):
-    fine = Mesh(mesh.devices.reshape(3, 4, 8, 2, 4), TOK + ("x",))
+    fine = Mesh(mesh.devices.reshape(3, 2, 2, 8, 2, 4), TOK + ("x",))
     return jax.shard_map(
         on_device,
         mesh=fine,

time: 153 us -> 145 us (0.948)
  waiting for transfers between devices: 6.58 us -> 0.62 us
    all_to_all x2 -> x1, starting transfers between devices: 12.8 us -> 4.84 us  [swap(): return lax.all_to_all(pieces, axis, 0, 0, tiled=True)]
    ppermute x0 -> x1, starting transfers between devices: none -> 7.92 us  [on_device(): others = lax.ppermute(own, 'core', [(0, 1), (1, 0)])]
    all_to_all x2 -> x1, waiting for transfers between devices: 6.56 us -> 0.01 us  [swap(): return lax.all_to_all(pieces, axis, 0, 0, tiled=True)]
where the time goes in v4:
time: 145 us
  blocking collectives  85.3 us (59%)
  starting transfers between devices  23.9 us (16%)
  between operations  13.5 us (9%)
  Pallas kernels  12.1 us (8%)
  matrix products  6.39 us (4%)
  local copies, waits for them, and re-layouts  2.16 us (1%)
    all_to_all x6, blocking collectives, swap(): return lax.all_to_all(pieces, axis, 0, 0, tiled=True)  85.3 us
    pallas_call x1, Pallas kernels, inverse_factor(): pl.pallas_call(inverse_factor_kernel, out_shape=jax.ShapeDtypeStruct((K,...  12.1 us
    ppermute x1, starting transfers between devices, on_device(): other = lax.ppermute(given, 'core', [(0, 1), (1, 0)])  11.1 us
    ppermute x1, starting transfers between devices, on_device(): others = lax.ppermute(own, 'core', [(0, 1), (1, 0)])  7.92 us
    all_to_all x1, starting transfers between devices, swap(): return lax.all_to_all(pieces, axis, 0, 0, tiled=True)  4.84 us
    dot_general x1, matrix products, on_device(): lax.dot_general(whole, inverse, (((1,), (1,)), ((), ())), precision=lax.P...  3.59 us
  transfers between devices with their start and end apart: 4, of which 1 were waited for; matrix products, arithmetic and copies ran while one was open for 1% of the time, Pallas kernels for 8%

profile of v4, /device:TPU:1, one launch (start us, length us, event | category | flops | bytes accessed | tf_op | source)
XLA Modules:
  0.0 144.8 jit_solution(7066682807453242546)
XLA Ops:
  6.5 0.0 copy-start
  6.5 1.2 copy-done
  7.8 1.7 %convolution_convert_fusion = bf16[256,256]{1,0:T(8,128)(2,1)S(1)} fusion(bf16[256,2048]{1,0:T(8,128)(2,1)S(1)} %copy-done, bf16[2048,256]{1,0:T(8,128)(2,1)} %param.3), kind=kOutput, calls=%fused_computation.5 | convolution fusion | flops 268500992 | bytes 2228224 | tf_op jit(solution)/shard_map/projected/dot_general | solution.py:111
  9.4 0.8 broadcast_in_dim.10
  10.3 4.8 %all-to-all-start = ((bf16[4,256,256]{2,1,0:T(8,128)(2,1)}), bf16[4,256,256]{2,1,0:T(8,128)(2,1)S(1)}, u32[]{:S(2)}, u32[]{:S(2)}) async-start(bf16[4,256,256]{2,1,0:T(8,128)(2,1)} %broadcast_in_dim.10), calls=%async_computation | async-start | bytes 1048576 | tf_op jit(solution)/shard_map/projected/all_to_all | solution.py:95
  15.1 0.0 all-gather.2.cloned.1.call-start
  15.1 11.1 %collective-permute-start = (bf16[256,1024]{1,0:T(8,128)(2,1)S(1)}, bf16[256,1024]{1,0:T(8,128)(2,1)S(1)}, u32[]{:S(2)}, u32[]{:S(2)}) collective-permute-start(bf16[256,1024]{1,0:T(8,128)(2,1)S(1)} %constant_dynamic-slice_fusion.1), channel_id=1, source_target_pairs={{0,4},{4,0},{1,5},{5,1},{2,6},{6,2},{3,7},{7,3},{8,12},{12,8},{9,1... | collective-permute-start | bytes 1572872 | tf_op jit(solution)/shard_map/ppermute | solution.py:108
  26.3 0.0 all-to-all-done
  26.3 0.1 convert_reduce_fusion.1
  26.4 7.9 %collective-permute-start.1 = (bf16[256,256]{1,0:T(8,128)(2,1)S(1)}, bf16[256,256]{1,0:T(8,128)(2,1)S(1)}, u32[]{:S(2)}, u32[]{:S(2)}) collective-permute-start(bf16[256,256]{1,0:T(8,128)(2,1)S(1)} %multiply_convert_fusion), channel_id=1, source_target_pairs={{0,4},{4,0},{1,5},{5,1},{2,6},{6,2},{3,7},{7,3},{8,12},{12,8},{9,1... | collective-permute-start | bytes 393224 | tf_op jit(solution)/shard_map/projected/ppermute | solution.py:114
  34.3 0.4 fusion.2
  34.7 0.6 collective-permute-done.1
  35.3 0.0 collective-permute-done
  35.3 0.4 fusion.1
  35.6 21.0 %all_to_all.35 = bf16[32,32,256]{2,1,0:T(8,128)(2,1)S(1)} all-to-all(bf16[32,32,256]{2,1,0:T(8,128)(2,1)S(1)} %bitcast.13), channel_id=1, replica_groups=mesh['zh'=3,'zm'=2,'zl'=2,'y'=8,'core'=2,'x'=4] {'y','zm','zl'}, dimensions={0} | all-to-all | bytes 1048576 | tf_op jit(solution)/shard_map/moment/all_to_all | solution.py:95
  56.7 0.1 convert_reduce_fusion
  56.8 17.6 %all_to_all.36 = f32[3,32,256]{2,1,0:T(8,128)S(1)} all-to-all(f32[3,32,256]{2,1,0:T(8,128)S(1)} %broadcast_in_dim.11), channel_id=1, replica_groups=mesh['zh'=3,'zm'=2,'zl'=2,'y'=8,'core'=2,'x'=4] {'zh'}, dimensions={0} | all-to-all | bytes 196608 | tf_op jit(solution)/shard_map/moment/all_to_all | solution.py:95
  74.4 9.8 %all_to_all.37 = f32[4,32,256]{2,1,0:T(8,128)S(1)} all-to-all(f32[4,32,256]{2,1,0:T(8,128)S(1)} %broadcast_in_dim.12), channel_id=1, replica_groups=mesh['zh'=3,'zm'=2,'zl'=2,'y'=8,'core'=2,'x'=4] {'zm','zl'}, dimensions={0} | all-to-all | bytes 262144 | tf_op jit(solution)/shard_map/moment/all_to_all | solution.py:95
  84.2 0.7 broadcast_multiply_fusion
  84.9 0.0 all-gather.2.cloned.1.call-update
  84.9 0.4 convolution_bitcast_fusion
  85.4 12.3 %all_to_all.38 = f32[8,16,256]{2,1,0:T(8,128)S(1)} all-to-all(f32[8,16,256]{2,1,0:T(8,128)S(1)} %bitcast.16), channel_id=1, replica_groups=mesh['zh'=3,'zm'=2,'zl'=2,'y'=8,'core'=2,'x'=4] {'core','x'}, dimensions={0} | all-to-all | bytes 262144 | tf_op jit(solution)/shard_map/gram/all_to_all | solution.py:95
  97.7 11.1 %all_to_all.39 = f32[8,16,256]{2,1,0:T(8,128)S(1)} all-to-all(f32[8,16,256]{2,1,0:T(8,128)S(1)} %broadcast_in_dim.13), channel_id=1, replica_groups=mesh['zh'=3,'zm'=2,'zl'=2,'y'=8,'core'=2,'x'=4] {'y'}, dimensions={0} | all-to-all | bytes 262144 | tf_op jit(solution)/shard_map/gram/all_to_all | solution.py:95
  108.8 13.5 %all_to_all.40 = f32[16,16,256]{2,1,0:T(8,128)} all-to-all(f32[16,16,256]{2,1,0:T(8,128)S(1)} %broadcast_in_dim.14), channel_id=1, replica_groups=mesh['zh'=3,'zm'=2,'zl'=2,'y'=8,'core'=2,'x'=4] {'zl','core','x'}, dimensions={0} | all-to-all | bytes 524288 | tf_op jit(solution)/shard_map/gram/all_to_all | solution.py:95
  122.3 12.1 %new_basis.1 = f32[256,256]{1,0:T(8,128)} custom-call(f32[256,256]{1,0:T(8,128)} %bitcast.14), custom_call_target="tpu_custom_call" | custom-call | flops 40000000 | bytes 524288 | tf_op jit(solution)/shard_map/new_basis/pallas_call | solution.py:84
  134.4 0.0 all-gather.2.cloned.1.call-done
  134.4 3.6 %fusion = bf16[2048,256]{1,0:T(8,128)(2,1)} fusion(f32[2048,256]{1,0:T(8,128)} %all-gather.2.cloned.1.call-done, f32[256,256]{1,0:T(8,128)} %new_basis.1), kind=kOutput, calls=%fused_computation.1 | convolution fusion | flops 806354944 | bytes 3407872 | tf_op jit(solution)/shard_map/new_basis/dot_general | solution.py:140
  (10 shorter events, 0.2 us)
Async XLA Ops:
  6.5 1.2 copy-start
  10.3 16.0 %all-to-all-start = ((bf16[4,256,256]{2,1,0:T(8,128)(2,1)}), bf16[4,256,256]{2,1,0:T(8,128)(2,1)S(1)}, u32[]{:S(2)}, u32[]{:S(2)}) async-start(bf16[4,256,256]{2,1,0:T(8,128)(2,1)} %broadcast_in_dim.10), calls=%async_computation | async-start | bytes 1048576 | tf_op jit(solution)/shard_map/projected/all_to_all | solution.py:95
  15.1 119.3 %all-gather.2.cloned.1.call-start = ((), (), s32[]{:S(2)}) async-start(), calls=%async_computation.7 | async-start | bytes 2228224 | tf_op jit(solution)/shard_map/moment/all_gather | solution.py:125
  15.1 20.1 %collective-permute-start = (bf16[256,1024]{1,0:T(8,128)(2,1)S(1)}, bf16[256,1024]{1,0:T(8,128)(2,1)S(1)}, u32[]{:S(2)}, u32[]{:S(2)}) collective-permute-start(bf16[256,1024]{1,0:T(8,128)(2,1)S(1)} %constant_dynamic-slice_fusion.1), channel_id=1, source_target_pairs={{0,4},{4,0},{1,5},{5,1},{2,6},{6,2},{3,7},{7,3},{8,12},{12,8},{9,1... | collective-permute-start | bytes 1572872 | tf_op jit(solution)/shard_map/ppermute | solution.py:108
  26.4 8.9 %collective-permute-start.1 = (bf16[256,256]{1,0:T(8,128)(2,1)S(1)}, bf16[256,256]{1,0:T(8,128)(2,1)S(1)}, u32[]{:S(2)}, u32[]{:S(2)}) collective-permute-start(bf16[256,256]{1,0:T(8,128)(2,1)S(1)} %multiply_convert_fusion), channel_id=1, source_target_pairs={{0,4},{4,0},{1,5},{5,1},{2,6},{6,2},{3,7},{7,3},{8,12},{12,8},{9,1... | collective-permute-start | bytes 393224 | tf_op jit(solution)/shard_map/projected/ppermute | solution.py:114
Sparse Core Ops, SparseCore 0:
  85.0 40.1 all-gather.1

commit v5 on v4

--- a/solution.py
+++ b/solution.py
@@ -120,8 +120,8 @@
         ) + lax.dot_general(other, others, over_tokens, preferred_element_type=jnp.float32)
         pieces = chip_sum.astype(jnp.bfloat16).reshape(32, half // 32, K)
         part = jnp.sum(swap(pieces, ("y", "zm", "zl")).astype(jnp.float32), axis=0)
-        part = jnp.sum(share(part, "zh"), axis=0)
-        moment = share(part, ("zm", "zl")).reshape(half // 8, K) / TOKENS
+        part = jnp.sum(share(part, "zh"), axis=0) / TOKENS
+        moment = share(part, ("zm", "zl")).reshape(half // 8, K)
         whole = lax.all_gather(moment, ("core", "y"), axis=0, tiled=True)
 
     with jax.named_scope("gram"):

time: 145 us -> 146 us (level)
  no operation moved by 1% of the time
where the time goes in v5:
time: 146 us; the launch traced here: 145 us
  blocking collectives  85.3 us (58%)
  starting transfers between devices  23.9 us (16%)
  between operations  13.5 us (9%)
  Pallas kernels  12.1 us (8%)
  matrix products  7.36 us (5%)
  local copies, waits for them, and re-layouts  2.16 us (1%)
    all_to_all x6, blocking collectives, swap(): return lax.all_to_all(pieces, axis, 0, 0, tiled=True)  85.3 us
    pallas_call x1, Pallas kernels, inverse_factor(): pl.pallas_call(inverse_factor_kernel, out_shape=jax.ShapeDtypeStruct((K,...  12.1 us
    ppermute x1, starting transfers between devices, on_device(): other = lax.ppermute(given, 'core', [(0, 1), (1, 0)])  11.1 us
    ppermute x1, starting transfers between devices, on_device(): others = lax.ppermute(own, 'core', [(0, 1), (1, 0)])  7.92 us
    all_to_all x1, starting transfers between devices, swap(): return lax.all_to_all(pieces, axis, 0, 0, tiled=True)  4.84 us
    dot_general x1, matrix products, on_device(): lax.dot_general(whole, inverse, (((1,), (1,)), ((), ())), precision=lax.P...  3.6 us
  transfers between devices with their start and end apart: 4, of which 1 were waited for; matrix products, arithmetic and copies ran while one was open for 1% of the time, Pallas kernels for 8%

profile of v5, /device:TPU:1, one launch (start us, length us, event | category | flops | bytes accessed | tf_op | source)
XLA Modules:
  0.0 145.1 jit_solution(4603795992075976299)
XLA Ops:
  6.5 0.0 copy-start
  6.5 1.2 copy-done
  7.8 1.7 %convolution_convert_fusion = bf16[256,256]{1,0:T(8,128)(2,1)S(1)} fusion(bf16[256,2048]{1,0:T(8,128)(2,1)S(1)} %copy-done, bf16[2048,256]{1,0:T(8,128)(2,1)} %param.3), kind=kOutput, calls=%fused_computation.5 | convolution fusion | flops 268500992 | bytes 2228224 | tf_op jit(solution)/shard_map/projected/dot_general | solution.py:111
  9.4 0.8 broadcast_in_dim.10
  10.3 4.8 %all-to-all-start = ((bf16[4,256,256]{2,1,0:T(8,128)(2,1)}), bf16[4,256,256]{2,1,0:T(8,128)(2,1)S(1)}, u32[]{:S(2)}, u32[]{:S(2)}) async-start(bf16[4,256,256]{2,1,0:T(8,128)(2,1)} %broadcast_in_dim.10), calls=%async_computation | async-start | bytes 1048576 | tf_op jit(solution)/shard_map/projected/all_to_all | solution.py:95
  15.1 0.0 all-gather.2.cloned.1.call-start
  15.1 11.1 %collective-permute-start = (bf16[256,1024]{1,0:T(8,128)(2,1)S(1)}, bf16[256,1024]{1,0:T(8,128)(2,1)S(1)}, u32[]{:S(2)}, u32[]{:S(2)}) collective-permute-start(bf16[256,1024]{1,0:T(8,128)(2,1)S(1)} %constant_dynamic-slice_fusion.1), channel_id=1, source_target_pairs={{0,4},{4,0},{1,5},{5,1},{2,6},{6,2},{3,7},{7,3},{8,12},{12,8},{9,1... | collective-permute-start | bytes 1572872 | tf_op jit(solution)/shard_map/ppermute | solution.py:108
  26.3 0.0 all-to-all-done
  26.3 0.1 convert_reduce_fusion.1
  26.4 7.9 %collective-permute-start.1 = (bf16[256,256]{1,0:T(8,128)(2,1)S(1)}, bf16[256,256]{1,0:T(8,128)(2,1)S(1)}, u32[]{:S(2)}, u32[]{:S(2)}) collective-permute-start(bf16[256,256]{1,0:T(8,128)(2,1)S(1)} %multiply_convert_fusion), channel_id=1, source_target_pairs={{0,4},{4,0},{1,5},{5,1},{2,6},{6,2},{3,7},{7,3},{8,12},{12,8},{9,1... | collective-permute-start | bytes 393224 | tf_op jit(solution)/shard_map/projected/ppermute | solution.py:114
  34.3 0.4 fusion.2
  34.7 0.6 collective-permute-done.1
  35.3 0.0 collective-permute-done
  35.3 0.4 fusion.1
  35.6 21.0 %all_to_all.35 = bf16[32,32,256]{2,1,0:T(8,128)(2,1)S(1)} all-to-all(bf16[32,32,256]{2,1,0:T(8,128)(2,1)S(1)} %bitcast.15), channel_id=1, replica_groups=mesh['zh'=3,'zm'=2,'zl'=2,'y'=8,'core'=2,'x'=4] {'y','zm','zl'}, dimensions={0} | all-to-all | bytes 1048576 | tf_op jit(solution)/shard_map/moment/all_to_all | solution.py:95
  56.7 0.1 convert_reduce_fusion
  56.8 17.6 %all_to_all.36 = f32[3,32,256]{2,1,0:T(8,128)S(1)} all-to-all(f32[3,32,256]{2,1,0:T(8,128)S(1)} %broadcast_in_dim.11), channel_id=1, replica_groups=mesh['zh'=3,'zm'=2,'zl'=2,'y'=8,'core'=2,'x'=4] {'zh'}, dimensions={0} | all-to-all | bytes 196608 | tf_op jit(solution)/shard_map/moment/all_to_all | solution.py:95
  74.4 9.9 %all_to_all.37 = f32[4,32,256]{2,1,0:T(8,128)} all-to-all(f32[4,32,256]{2,1,0:T(8,128)S(1)} %broadcast_in_dim.12), channel_id=1, replica_groups=mesh['zh'=3,'zm'=2,'zl'=2,'y'=8,'core'=2,'x'=4] {'zm','zl'}, dimensions={0} | all-to-all | bytes 262144 | tf_op jit(solution)/shard_map/moment/all_to_all | solution.py:95
  84.3 0.0 all-gather.2.cloned.1.call-update
  84.4 1.4 convolution_bitcast_fusion
  85.8 12.3 %all_to_all.38 = f32[8,16,256]{2,1,0:T(8,128)S(1)} all-to-all(f32[8,16,256]{2,1,0:T(8,128)S(1)} %bitcast.18), channel_id=1, replica_groups=mesh['zh'=3,'zm'=2,'zl'=2,'y'=8,'core'=2,'x'=4] {'core','x'}, dimensions={0} | all-to-all | bytes 262144 | tf_op jit(solution)/shard_map/gram/all_to_all | solution.py:95
  98.1 11.6 %all_to_all.39 = f32[8,16,256]{2,1,0:T(8,128)S(1)} all-to-all(f32[8,16,256]{2,1,0:T(8,128)S(1)} %broadcast_in_dim.13), channel_id=1, replica_groups=mesh['zh'=3,'zm'=2,'zl'=2,'y'=8,'core'=2,'x'=4] {'y'}, dimensions={0} | all-to-all | bytes 262144 | tf_op jit(solution)/shard_map/gram/all_to_all | solution.py:95
  109.8 12.8 %all_to_all.40 = f32[16,16,256]{2,1,0:T(8,128)} all-to-all(f32[16,16,256]{2,1,0:T(8,128)S(1)} %broadcast_in_dim.14), channel_id=1, replica_groups=mesh['zh'=3,'zm'=2,'zl'=2,'y'=8,'core'=2,'x'=4] {'zl','core','x'}, dimensions={0} | all-to-all | bytes 524288 | tf_op jit(solution)/shard_map/gram/all_to_all | solution.py:95
  122.6 12.1 %new_basis.1 = f32[256,256]{1,0:T(8,128)} custom-call(f32[256,256]{1,0:T(8,128)} %bitcast.17), custom_call_target="tpu_custom_call" | custom-call | flops 40000000 | bytes 524288 | tf_op jit(solution)/shard_map/new_basis/pallas_call | solution.py:84
  134.7 0.0 all-gather.2.cloned.1.call-done
  134.7 3.6 %fusion = bf16[2048,256]{1,0:T(8,128)(2,1)} fusion(f32[2048,256]{1,0:T(8,128)} %all-gather.2.cloned.1.call-done, f32[256,256]{1,0:T(8,128)} %new_basis.1), kind=kOutput, calls=%fused_computation.1 | convolution fusion | flops 806354944 | bytes 3407872 | tf_op jit(solution)/shard_map/new_basis/dot_general | solution.py:140
  (11 shorter events, 0.2 us)
Async XLA Ops:
  6.5 1.2 copy-start
  10.3 16.0 %all-to-all-start = ((bf16[4,256,256]{2,1,0:T(8,128)(2,1)}), bf16[4,256,256]{2,1,0:T(8,128)(2,1)S(1)}, u32[]{:S(2)}, u32[]{:S(2)}) async-start(bf16[4,256,256]{2,1,0:T(8,128)(2,1)} %broadcast_in_dim.10), calls=%async_computation | async-start | bytes 1048576 | tf_op jit(solution)/shard_map/projected/all_to_all | solution.py:95
  15.1 119.6 %all-gather.2.cloned.1.call-start = ((), (), s32[]{:S(2)}) async-start(), calls=%async_computation.7 | async-start | bytes 2228224 | tf_op jit(solution)/shard_map/moment/all_gather | solution.py:125
  15.1 20.1 %collective-permute-start = (bf16[256,1024]{1,0:T(8,128)(2,1)S(1)}, bf16[256,1024]{1,0:T(8,128)(2,1)S(1)}, u32[]{:S(2)}, u32[]{:S(2)}) collective-permute-start(bf16[256,1024]{1,0:T(8,128)(2,1)S(1)} %constant_dynamic-slice_fusion.1), channel_id=1, source_target_pairs={{0,4},{4,0},{1,5},{5,1},{2,6},{6,2},{3,7},{7,3},{8,12},{12,8},{9,1... | collective-permute-start | bytes 1572872 | tf_op jit(solution)/shard_map/ppermute | solution.py:108
  26.4 8.9 %collective-permute-start.1 = (bf16[256,256]{1,0:T(8,128)(2,1)S(1)}, bf16[256,256]{1,0:T(8,128)(2,1)S(1)}, u32[]{:S(2)}, u32[]{:S(2)}) collective-permute-start(bf16[256,256]{1,0:T(8,128)(2,1)S(1)} %multiply_convert_fusion), channel_id=1, source_target_pairs={{0,4},{4,0},{1,5},{5,1},{2,6},{6,2},{3,7},{7,3},{8,12},{12,8},{9,1... | collective-permute-start | bytes 393224 | tf_op jit(solution)/shard_map/projected/ppermute | solution.py:114
Sparse Core Ops, SparseCore 0:
  84.5 40.7 all-gather.1
